TPU v7x, 128 devices: a whole 4x4x4 slice. The times are simulated.
128 devices in a mesh: gx: 8 (over x_hi, z), gy: 8 (over y, x_lo), dp: 2 (over core).
Axes of the slice: x: 4 (x_hi: 2, x_lo: 2; x = x_hi * 2 + x_lo), y: 4, z: 4, core: 2. Of those that a mesh axis runs over, the one named last changes fastest.
Arguments:
- inputs: bfloat16 [4, 4, 64, 128, 128], P('dp', None, 'gx', 'gy'), may hold values from -6 to 6
- cotangent: bfloat16 [4, 64, 16, 32, 32], P('dp', None, 'gx', 'gy'), may hold values from -96 to 96
- w_first: bfloat16 [32, 4, 3, 3, 3], replicated, may hold values from -0.625 to 0.625
- w_second: bfloat16 [64, 32, 3, 3, 3], replicated, may hold values from -0.21875 to 0.21875
- b_first: float32 [32], replicated, may hold values from -3 to 3
- b_second: float32 [64], replicated, may hold values from -3 to 3
Outputs:
- grad_input: bfloat16 [4, 4, 64, 128, 128], P('dp', None, 'gx', 'gy')
- grad_w1: float32 [3456], P(('gx', 'gy', 'dp'))
- grad_w2: float32 [55296], P(('gx', 'gy', 'dp'))
All inputs are finite; a program needn't handle non-finite values.
Results may differ from a plain program's by a relative error of at most 0.014.
Values may be sent and summed in bfloat16 or wider, within the bound.
A program may use at most 192 MiB of HBM per device.

v0:
```python
import jax
import jax.numpy as jnp
from jax import lax
from jax.sharding import PartitionSpec as P


def extended(x, sides, width):
    for axis, dim in sides:
        size, length = (lax.axis_size(axis), x.shape[dim])
        up = [(i, (i + 1) % size) for i in range(size - 1)]
        down = [(j, i) for i, j in up]
        last = lax.slice_in_dim(x, length - width, length, axis=dim)
        initial = lax.slice_in_dim(x, 0, width, axis=dim)
        before = lax.ppermute(last, axis, up)
        after = lax.ppermute(initial, axis, down)
        x = jnp.concatenate([before, x, after], axis=dim)
    return x


def leaky_smooth(values):
    return 0.3 * values + 0.7 * values * jax.nn.sigmoid(values)


def leaky_slope(values):
    sig = jax.nn.sigmoid(values)
    return 0.3 + 0.7 * (sig + values * sig * (1.0 - sig))


def average_pool(values):
    count, chans, height, width, depth = values.shape
    blocks = values.reshape(count, chans, height // 2, 2, width // 2, 2, depth // 2, 2)
    return jnp.mean(blocks, axis=(3, 5, 7))


def spread_back(values):
    count, chans, height, width, depth = values.shape
    wide = jnp.broadcast_to(
        values[:, :, :, None, :, None, :, None], (count, chans, height, 2, width, 2, depth, 2)
    )
    return wide.reshape(count, chans, 2 * height, 2 * width, 2 * depth) * 0.125


def conv_cells(values, kernel, layout, margin):
    return lax.conv_general_dilated(
        values,
        kernel,
        (1, 1, 1),
        [(margin, margin), (margin, margin), (1, 1)],
        dimension_numbers=("NCDHW", layout, "NCDHW"),
        preferred_element_type=jnp.float32,
    )


def tap_grads(padded, grads):
    result = lax.conv_general_dilated(
        padded,
        grads,
        (1, 1, 1),
        [(0, 0), (0, 0), (1, 1)],
        dimension_numbers=("CNDHW", "IODHW", "NCDHW"),
        preferred_element_type=jnp.float32,
    )
    return jnp.transpose(result, (1, 0, 2, 3, 4))


def on_device(inputs, cotangent, w_first, w_second, b_first, b_second):
    padded_in = extended(inputs, (("gx", 2), ("gy", 3)), 1)
    pre_first = conv_cells(padded_in, w_first, "OIDHW", 0) + b_first[None, :, None, None, None]
    pooled = average_pool(leaky_smooth(pre_first)).astype(jnp.bfloat16)
    padded_pool = extended(pooled, (("gx", 2), ("gy", 3)), 1)
    pre_second = conv_cells(padded_pool, w_second, "OIDHW", 0) + b_second[None, :, None, None, None]
    grad_second = (leaky_slope(pre_second) * spread_back(cotangent.astype(jnp.float32))).astype(
        jnp.bfloat16
    )
    second_terms = tap_grads(padded_pool, grad_second)
    padded_grad = extended(grad_second, (("gx", 2), ("gy", 3)), 1)
    flip_second = jnp.flip(w_second, (2, 3, 4))
    grad_pooled = conv_cells(padded_grad, flip_second, "IODHW", 0)
    grad_first = (leaky_slope(pre_first) * spread_back(grad_pooled)).astype(jnp.bfloat16)
    first_terms = tap_grads(padded_in, grad_first)
    flip_first = jnp.flip(w_first, (2, 3, 4))
    padded_first = extended(grad_first, (("gx", 2), ("gy", 3)), 1)
    grad_input = conv_cells(padded_first, flip_first, "IODHW", 0).astype(jnp.bfloat16)
    devices = lax.axis_size(("gx", "gy", "dp"))
    cells = devices * inputs.shape[0] * inputs.shape[2] * inputs.shape[3] * inputs.shape[4]
    first_rows = (first_terms * (1.0 / cells**0.5)).reshape(devices, -1)
    second_rows = (second_terms * (1.0 / (cells / 8) ** 0.5)).reshape(devices, -1)
    split_at = first_rows.shape[1]
    stacked_rows = jnp.concatenate([first_rows, second_rows], axis=1)
    owned = lax.psum_scatter(stacked_rows, ("gx", "gy", "dp"), scatter_dimension=0, tiled=True)
    grad_w1 = owned[0, :split_at]
    grad_w2 = owned[0, split_at:]
    return (grad_input, grad_w1, grad_w2)


def solution(mesh):
    return jax.shard_map(
        on_device,
        mesh=mesh,
        in_specs=(
            P("dp", None, "gx", "gy", None),
            P("dp", None, "gx", "gy", None),
            P(),
            P(),
            P(),
            P(),
        ),
        out_specs=(P("dp", None, "gx", "gy", None), P(("gx", "gy", "dp")), P(("gx", "gy", "dp"))),
        check_vma=False,
    )
```

profile of v0, /device:TPU:0, one launch (start us, length us, event | category | flops | bytes accessed | tf_op | source)
XLA Modules:
  0.0 991.1 jit_solution(11699998865240017732)
XLA Ops:
  22.6 11.6 %copy.144 = bf16[2,4,10,16,128]{1,0,4,3,2:T(2,128)(2,1)} copy(bf16[2,4,10,16,128]{4,3,2,1,0:T(8,128)(2,1)S(1)} %constant_dynamic-update-slice_fusion) | data formatting | bytes 655360 | tf_op jit(solution)/shard_map/concatenate | solution.py:16
  35.3 36.7 %fusion.60 = bf16[4,10,18,2,128]{0,3,4,2,1:T(2,128)(2,1)S(1)} fusion(bf16[2,4,10,1,128]{1,0,4,3,2:T(2,128)(2,1)S(1)} %copy.145, bf16[2,4,10,16,128]{1,0,4,3,2:T(2,128)(2,1)} %copy.144, bf16[2,4,10,1,128]{1,0,4,3,2:T(2,128)(2,1)S(1)} %copy.143), kind=kLoop, calls=%fused_computation.79 | loop fusion | flops 368640 | bytes 737280 | tf_op jit(solution)/shard_map/concatenate | solution.py:16
  72.0 15.1 %pad = bf16[4,10,18,2,136]{0,3,4,2,1:T(2,128)(2,1)} pad(bf16[4,10,18,2,128]{0,3,4,2,1:T(2,128)(2,1)S(1)} %fusion.60, bf16[]{:T(256)} %constant.4), padding=0_0x0_0x0_0x0_0x1_7 | pad | bytes 760322 | tf_op jit(solution)/shard_map/concatenate | solution.py:16
  87.1 30.2 %copy.174 = bf16[4,10,18,2,8,17]{5,4,3,2,1,0:T(8,128)(2,1)S(1)} copy(bf16[4,10,18,2,8,17]{0,3,5,4,2,1:T(2,128)(2,1)} %bitcast.84) | data formatting | bytes 783360 | tf_op jit(solution)/shard_map/conv_general_dilated | solution.py:44
  121.6 8.8 copy.147
  130.5 31.6 %multiply_add_fusion = (f32[8,16,16,17,32]{4,2,3,1,0:T(8,128)}, f32[8,16,16,17,32]{4,2,3,1,0:T(8,128)S(1)}) fusion(f32[32]{0:T(128)S(1)} %copy-done.19, pred[16,17]{0,1:T(8,128)(4,1)S(1)} %copy-done.21, bf16[4,10,18,16,19]{3,0,4,2,1:T(4,128)(2,1)} %copy.147, bf16[32,4,3,3,3]{0,1,4,3,2:T(4,128)(2,1)S(1)} %copy-done.17), kind=kOutput, calls=%fused_computation.1 | convolution fusion | flops 257359872 | bytes 9357968 | tf_op jit(solution)/shard_map/conv_general_dilated | solution.py:44
  162.1 6.3 copy.149
  174.6 12.4 %reduce_sum.9 = f32[2,32,4,8,64]{1,3,4,0,2:T(8,128)S(1)} reduce(f32[2,32,4,2,8,2,64,2]{1,5,4,7,6,0,3,2:T(2,128)} %bitcast.80, f32[]{:T(128)} %constant.10.clone.1), dimensions={3,5,7}, to_apply=%region_0.0 | reduce | flops 917504 | bytes 4718596 | tf_op jit(solution)/shard_map/reduce_sum | solution.py:32
  229.0 7.7 collective-permute-start.8
  238.2 37.5 %fusion.64 = bf16[2,4,10,18,128]{1,0,4,3,2:T(2,128)(2,1)} fusion(bf16[2,4,10,1,128]{1,0,4,3,2:T(2,128)(2,1)} %copy-done.7, bf16[2,4,10,16,128]{1,0,4,3,2:T(2,128)(2,1)S(1)} %bitcast.75, bf16[2,4,10,1,128]{1,0,4,3,2:T(2,128)(2,1)S(1)} %copy-done.6), kind=kLoop, calls=%bitcast_fusion.2.clone.1 | loop fusion | flops 368640 | bytes 737280 | tf_op jit(solution)/shard_map/transpose | solution.py:63
  275.8 8.2 copy.148
  292.1 15.5 %convolution_multiply_fusion = f32[64,32,3,3,3]{0,1,4,3,2:T(8,128)S(1)} fusion(bf16[2,64,4,8,64]{1,3,4,0,2:T(8,128)(2,1)S(1)} %fusion.28, bf16[2,32,6,1,64]{1,0,4,3,2:T(2,128)(2,1)S(1)} %copy-done.14, bf16[2,32,1,8,64]{1,0,4,3,2:T(2,128)(2,1)S(1)} %copy-done.10, bf16[2,32,4,8,64]{1,0,4,3,2:T(2,128)(2,1)S(1)} %copy-done.4, ...), kind=kOutput, calls=%fused_computation.50 | convolution fusion | flops 450779136 | bytes 1236992 | tf_op jit(solution)/shard_map/transpose | solution.py:63
  307.6 12.1 %copy.171 = f32[64,32,3,3,3]{4,3,2,1,0:T(4,128)} copy(f32[64,32,3,3,3]{0,1,4,3,2:T(8,128)S(1)} %convolution_multiply_fusion) | data formatting | bytes 442368 | tf_op jit(solution)/shard_map/mul | solution.py:87
  319.7 11.9 %reshape.27 = f32[128,432]{1,0:T(8,128)} reshape(f32[64,32,3,3,3]{4,3,2,1,0:T(4,128)} %copy.171) | data formatting | bytes 442368 | tf_op jit(solution)/shard_map/reshape | solution.py:87
  336.7 9.1 select_multiply_fusion
  346.7 7.3 broadcast_in_dim.5
  354.0 9.7 fusion.1
  375.5 87.8 %fusion.36 = f32[32,4,3,3,3]{0,1,4,3,2:T(4,128)S(1)} fusion(bf16[2,32,8,16,128]{1,3,4,0,2:T(8,128)(2,1)} %fusion.1, bf16[2,4,10,18,128]{1,0,4,3,2:T(2,128)(2,1)} %fusion.64), kind=kOutput, calls=%fused_computation.51 | convolution fusion | flops 225316224 | bytes 2479616 | tf_op jit(solution)/shard_map/transpose | solution.py:63
  488.9 125.4 %all-reduce.3.cloned.1.call-done = f32[128,459]{1,0:T(8,128)} async-done(((f32[128,459]{1,0:T(8,128)}), f32[128,459]{1,0:T(8,128)}) %all-reduce.3.cloned.1.call-update) | async-done | bytes 235024
  616.9 12.0 %copy.164 = bf16[2,32,10,16,128]{4,1,3,2,0:T(8,128)(2,1)} copy(bf16[2,32,10,16,128]{1,3,4,0,2:T(8,128)(2,1)} %copy-done.2) | data formatting | bytes 5242880 | tf_op jit(solution)/shard_map/concatenate | solution.py:16
  630.9 17.4 %copy.177 = bf16[32,10,18,2,128]{0,3,4,2,1:T(2,128)(2,1)} copy(bf16[32,10,18,2,128]{4,0,2,1,3:T(8,128)(2,1)S(1)} %maximum_bitcast_fusion.1) | data formatting | bytes 5898240
  648.4 15.5 %pad.6.clone = bf16[32,10,18,2,136]{0,3,4,2,1:T(2,128)(2,1)S(1)} pad(bf16[32,10,18,2,128]{0,3,4,2,1:T(2,128)(2,1)} %copy.177, bf16[]{:T(256)} %constant.4), padding=0_0x0_0x0_0x0_0x1_7 | pad | bytes 6082562 | tf_op jit(solution)/shard_map/concatenate | solution.py:16
  664.7 15.7 %fusion.2 = bf16[32,10,18,2,8,19]{0,3,5,4,2,1:T(2,128)(2,1)S(1)} fusion(bf16[32,10,18,2,7,2]{0,3,5,4,2,1:T(2,128)(2,1)S(1)} %slice.98, bf16[32,10,18,2,8,17]{0,3,5,4,2,1:T(2,128)(2,1)S(1)} %bitcast.83), kind=kLoop, calls=%fused_computation.8 | loop fusion | flops 10506240 | bytes 6958080 | tf_op jit(solution)/shard_map/conv_general_dilated | solution.py:44
  680.5 290.8 %fusion.3 = bf16[8,16,16,17,4]{2,4,3,1,0:T(4,128)(2,1)} fusion(bf16[32,4,3,3,3]{0,1,4,3,2:T(4,128)(2,1)S(1)} %copy-done.18, bf16[32,10,18,2,8,19]{0,3,5,4,2,1:T(2,128)(2,1)S(1)} %fusion.2), kind=kOutput, calls=%fused_computation.9 | convolution fusion | flops 240648192 | bytes 3787520 | tf_op jit(solution)/shard_map/conv_general_dilated | solution.py:44
  (163 shorter events, 139.3 us)
Async XLA Ops:
  7.2 214.7 %copy-start = (bf16[64,32,3,3,3]{0,1,4,3,2:T(8,128)(2,1)S(1)}, bf16[64,32,3,3,3]{0,1,4,3,2:T(8,128)(2,1)}, u32[]{:S(2)}) copy-start(bf16[64,32,3,3,3]{0,1,4,3,2:T(8,128)(2,1)} %param.9) | copy-start | bytes 331780
  7.2 607.1 %all-reduce.3.cloned.1.call-start = ((), (), s32[]{:S(2)}) async-start(), calls=%async_computation | async-start | bytes 524288
  8.1 5.5 collective-permute-start
  12.0 5.8 collective-permute-start.1
  17.9 16.3 %collective-permute-start.2 = (bf16[2,4,10,1,128]{4,1,3,2,0:T(4,128)(2,1)S(1)}, bf16[2,4,10,1,128]{4,1,3,2,0:T(4,128)(2,1)S(1)}, u32[]{:S(2)}, u32[]{:S(2)}) collective-permute-start(bf16[2,4,10,1,128]{4,1,3,2,0:T(4,128)(2,1)S(1)} %copy.175), channel_id=1, source_target_pairs={{0,2},{2,4},{4,6},{6,8},{8,10},{10,12},{12,14},{1,3},{3,5},{5,7},{... | collective-permute-start | bytes 61448 | tf_op jit(solution)/shard_map/ppermute | solution.py:14
  21.3 13.4 %collective-permute-start.3 = (bf16[2,4,10,1,128]{4,1,3,2,0:T(4,128)(2,1)S(1)}, bf16[2,4,10,1,128]{4,1,3,2,0:T(4,128)(2,1)S(1)}, u32[]{:S(2)}, u32[]{:S(2)}) collective-permute-start(bf16[2,4,10,1,128]{4,1,3,2,0:T(4,128)(2,1)S(1)} %copy.176), channel_id=1, source_target_pairs={{2,0},{4,2},{6,4},{8,6},{10,8},{12,10},{14,12},{3,1},{5,3},{7,5},{... | collective-permute-start | bytes 61448 | tf_op jit(solution)/shard_map/ppermute | solution.py:15
  189.2 7.7 collective-permute-start.4
  193.0 8.3 collective-permute-start.5
  202.0 7.7 collective-permute-start.6
  206.5 8.2 collective-permute-start.7
  221.9 53.8 %slice-start.8 = ((s8[17825792]{0:T(1024)(128)(4,1)}), s8[4194304]{0:T(1024)(128)(4,1)S(1)}, s32[]{:S(2)}) async-start(s8[17825792]{0:T(1024)(128)(4,1)} %bitcast.85), calls=%async_computation.9 | async-start | bytes 8388608
  221.9 53.8 %slice-start.9 = ((s8[17825792]{0:T(1024)(128)(4,1)}), s8[4194304]{0:T(1024)(128)(4,1)S(1)}, s32[]{:S(2)}) async-start(s8[17825792]{0:T(1024)(128)(4,1)} %bitcast.85), calls=%async_computation.10 | async-start | bytes 8388608
  221.9 53.8 %slice-start.10 = ((s8[17825792]{0:T(1024)(128)(4,1)}), s8[4194304]{0:T(1024)(128)(4,1)S(1)}, s32[]{:S(2)}) async-start(s8[17825792]{0:T(1024)(128)(4,1)} %bitcast.85), calls=%async_computation.11 | async-start | bytes 8388608
  226.6 49.1 %slice-start.11 = ((s8[17825792]{0:T(1024)(128)(4,1)}), s8[4194304]{0:T(1024)(128)(4,1)S(1)}, s32[]{:S(2)}) async-start(s8[17825792]{0:T(1024)(128)(4,1)} %bitcast.85), calls=%async_computation.12 | async-start | bytes 8388608
  229.0 55.1 %collective-permute-start.8 = (bf16[2,64,1,8,64]{1,3,4,0,2:T(8,128)(2,1)}, bf16[2,64,1,8,64]{1,3,4,0,2:T(8,128)(2,1)}, u32[]{:S(2)}, u32[]{:S(2)}) collective-permute-start(bf16[2,64,1,8,64]{1,3,4,0,2:T(8,128)(2,1)} %get-tuple-element.28), channel_id=1, source_target_pairs={{0,16},{16,32},{32,48},{48,64},{64,80},{80,96},{96,112},{1,17},{17... | collective-permute-start | bytes 393224 | tf_op jit(solution)/shard_map/ppermute | solution.py:14
  236.7 39.0 %slice-start.12 = ((s8[17825792]{0:T(1024)(128)(4,1)}), s8[1048576]{0:T(1024)(128)(4,1)S(1)}, s32[]{:S(2)}) async-start(s8[17825792]{0:T(1024)(128)(4,1)} %bitcast.85), calls=%async_computation.13 | async-start | bytes 2097152
  236.7 47.3 %collective-permute-start.9 = (bf16[2,64,1,8,64]{1,3,4,0,2:T(8,128)(2,1)}, bf16[2,64,1,8,64]{1,3,4,0,2:T(8,128)(2,1)}, u32[]{:S(2)}, u32[]{:S(2)}) collective-permute-start(bf16[2,64,1,8,64]{1,3,4,0,2:T(8,128)(2,1)} %get-tuple-element.29), channel_id=1, source_target_pairs={{16,0},{32,16},{48,32},{64,48},{80,64},{96,80},{112,96},{17,1},{33... | collective-permute-start | bytes 393224 | tf_op jit(solution)/shard_map/ppermute | solution.py:15
  285.9 45.8 %collective-permute-start.10 = (bf16[2,64,6,1,64]{1,3,4,0,2:T(2,128)(2,1)S(1)}, bf16[2,64,6,1,64]{1,3,4,0,2:T(2,128)(2,1)S(1)}, u32[]{:S(2)}, u32[]{:S(2)}) collective-permute-start(bf16[2,64,6,1,64]{1,3,4,0,2:T(2,128)(2,1)S(1)} %get-tuple-element.24), channel_id=1, source_target_pairs={{0,2},{2,4},{4,6},{6,8},{8,10},{10,12},{12,14},{1,3},{3,5},{5,7},{... | collective-permute-start | bytes 294920 | tf_op jit(solution)/shard_map/ppermute | solution.py:14
  290.6 41.1 %collective-permute-start.11 = (bf16[2,64,6,1,64]{1,3,4,0,2:T(2,128)(2,1)S(1)}, bf16[2,64,6,1,64]{1,3,4,0,2:T(2,128)(2,1)}, u32[]{:S(2)}, u32[]{:S(2)}) collective-permute-start(bf16[2,64,6,1,64]{1,3,4,0,2:T(2,128)(2,1)S(1)} %get-tuple-element.25), channel_id=1, source_target_pairs={{2,0},{4,2},{6,4},{8,6},{10,8},{12,10},{14,12},{3,1},{5,3},{7,5},{... | collective-permute-start | bytes 294920 | tf_op jit(solution)/shard_map/ppermute | solution.py:15
  367.3 97.5 %collective-permute-start.12 = (bf16[2,32,1,16,128]{4,3,2,1,0:T(8,128)(2,1)}, bf16[2,32,1,16,128]{4,3,2,1,0:T(8,128)(2,1)}, u32[]{:S(2)}, u32[]{:S(2)}) collective-permute-start(bf16[2,32,1,16,128]{4,3,2,1,0:T(8,128)(2,1)} %copy.158), channel_id=1, source_target_pairs={{0,16},{16,32},{32,48},{48,64},{64,80},{80,96},{96,112},{1,17},{17... | collective-permute-start | bytes 786440 | tf_op jit(solution)/shard_map/ppermute | solution.py:14
  374.2 92.5 %collective-permute-start.13 = (bf16[2,32,1,16,128]{4,3,2,1,0:T(8,128)(2,1)}, bf16[2,32,1,16,128]{4,3,2,1,0:T(8,128)(2,1)}, u32[]{:S(2)}, u32[]{:S(2)}) collective-permute-start(bf16[2,32,1,16,128]{4,3,2,1,0:T(8,128)(2,1)} %copy.159), channel_id=1, source_target_pairs={{16,0},{32,16},{48,32},{64,48},{80,64},{96,80},{112,96},{17,1},{33... | collective-permute-start | bytes 786440 | tf_op jit(solution)/shard_map/ppermute | solution.py:15
  375.5 88.5 %copy-start.8 = (f32[128,432]{1,0:T(8,128)S(1)}, f32[128,432]{1,0:T(8,128)}, u32[]{:S(2)}) copy-start(f32[128,432]{1,0:T(8,128)} %reshape.27) | copy-start | bytes 663556
  482.4 146.5 %collective-permute-start.14 = (bf16[2,32,10,1,128]{4,1,3,2,0:T(8,128)(2,1)S(1)}, bf16[2,32,10,1,128]{4,1,3,2,0:T(8,128)(2,1)S(1)}, u32[]{:S(2)}, u32[]{:S(2)}) collective-permute-start(bf16[2,32,10,1,128]{4,1,3,2,0:T(8,128)(2,1)S(1)} %copy.162), channel_id=1, source_target_pairs={{0,2},{2,4},{4,6},{6,8},{8,10},{10,12},{12,14},{1,3},{3,5},{5,7},{... | collective-permute-start | bytes 491528 | tf_op jit(solution)/shard_map/ppermute | solution.py:14
  487.6 141.2 %collective-permute-start.15 = (bf16[2,32,10,1,128]{4,1,3,2,0:T(8,128)(2,1)S(1)}, bf16[2,32,10,1,128]{4,1,3,2,0:T(8,128)(2,1)S(1)}, u32[]{:S(2)}, u32[]{:S(2)}) collective-permute-start(bf16[2,32,10,1,128]{4,1,3,2,0:T(8,128)(2,1)S(1)} %copy.163), channel_id=1, source_target_pairs={{2,0},{4,2},{6,4},{8,6},{10,8},{12,10},{14,12},{3,1},{5,3},{7,5},{... | collective-permute-start | bytes 491528 | tf_op jit(solution)/shard_map/ppermute | solution.py:15
  (29 other events, 430.9 us)
Sparse Core Ops, SparseCore 0:
  464.9 149.3 all-reduce.2
where the time goes:
time: 999 us; the launch traced here: 991 us
  matrix products  440 us (44%)
  local copies, waits for them, and re-layouts  206 us (21%)
  waiting for transfers between devices  143 us (14%)
  other arithmetic  139 us (14%)
  starting transfers between devices  48.5 us (5%)
  between operations  15.4 us (2%)
    conv_general_dilated x4, matrix products, conv_cells(): lax.conv_general_dilated(values, kernel, (1, 1, 1), [(margin, margin), (m...  336 us
    unnamed x2, waiting for transfers between devices  125 us
    transpose x2, matrix products, tap_grads(): return jnp.transpose(result, (1, 0, 2, 3, 4))  103 us
    concatenate x7, local copies, waits for them, and re-layouts, extended(): x = jnp.concatenate([before, x, after], axis=dim)  57.1 us
    concatenate x5, other arithmetic, extended(): x = jnp.concatenate([before, x, after], axis=dim)  52.6 us
    conv_general_dilated x9, local copies, waits for them, and re-layouts, conv_cells(): lax.conv_general_dilated(values, kernel, (1, 1, 1), [(margin, margin), (m...  47.9 us
    ppermute x8, starting transfers between devices, extended(): before = lax.ppermute(last, axis, up)  37.9 us
    transpose x1, other arithmetic, tap_grads(): return jnp.transpose(result, (1, 0, 2, 3, 4))  37.5 us
  transfers between devices with their start and end apart: 17, of which 7 were waited for; matrix products, arithmetic and copies ran while one was open for 22% of the time, Pallas kernels for 0%

commit v1 on v0

v1 whole, which is shorter than its diff:
```python
import functools

import jax
import jax.numpy as jnp
import ml_dtypes
import numpy as np
from jax import lax
from jax.experimental import pallas as pl
from jax.experimental.pallas import tpu as pltpu
from jax.sharding import PartitionSpec as P

MESH = pl.DeviceIdType.MESH
F32 = jnp.float32
BF16 = jnp.bfloat16
DIRS = [(0, 1), (0, -1), (1, 0), (-1, 0), (1, 1), (1, -1), (-1, 1), (-1, -1)]
CELLS = 4194304


def constants():
    depth_map = np.zeros((256, 768), np.float32)
    for n in range(2):
        for z in range(128):
            lane = (z % 2) * 128 + (z // 2 % 2) * 64 + n * 32 + z // 4
            for t in range(3):
                src = z + t - 1
                if 0 <= src < 128:
                    depth_map[n * 128 + src, t * 256 + lane] = 1
    restore = depth_map[:, 256:512].T.copy()
    pool_map = np.zeros((128, 256), np.float32)
    for n in range(2):
        for z in range(64):
            lane = (z % 2) * 64 + n * 32 + z // 2
            for half, src in ((0, z - 1), (1, z + 1)):
                if 0 <= src < 64:
                    pool_map[(src % 2) * 64 + n * 32 + src // 2, half * 128 + lane] = 1
    cot_map = np.zeros((128, 256), np.float32)
    for h in range(2):
        for b in range(2):
            for n in range(2):
                for k in range(32):
                    cot_map[n * 64 + h * 32 + k, h * 128 + b * 64 + n * 32 + k] = 1
    row_of = {}
    place = np.full((80,), -100.0, np.float32)
    chan = np.full((80,), -1)
    for c in range(4):
        for y in range(-1, 17):
            row = 64 + c if y < 0 else 68 + c if y > 15 else c * 16 + y
            row_of[c, y] = row
            place[row] = y
            chan[row] = c
    toeplitz = np.zeros((16, 128, 720), np.float32)
    for r in range(16):
        y = 2 * (r % 8) + r // 8
        for dx in range(3):
            for dy in range(3):
                for dz in range(3):
                    for c in range(4):
                        tap = (dx * 3 + dy) * 3 + dz
                        toeplitz[r, tap * 4 + c, dx * 240 + dz * 80 + row_of[c, y + dy - 1]] = 1
    gather = np.zeros((3, 720, 128), np.float32)
    for dy in range(3):
        for dx in range(3):
            for dz in range(3):
                for row in range(72):
                    gather[dy, dx * 240 + dz * 80 + row, chan[row] * 32 + dx * 9 + dy * 3 + dz] = 1
    select = np.zeros((16, 64), np.float32)
    for c in range(4):
        select[c, c * 16 + 15] = 1
        select[4 + c, c * 16] = 1
    b16 = lambda v: v.astype(ml_dtypes.bfloat16)
    return (
        b16(depth_map), b16(restore), b16(pool_map), b16(cot_map), b16(toeplitz), b16(gather), b16(select),
        b16(np.eye(128, dtype=np.float32)), np.tile(place, 9)[None, :],
    )


def dot(a, b):
    return jnp.dot(a, b, preferred_element_type=F32)


def dot_nt(a, b):
    return lax.dot_general(a, b, (((1,), (1,)), ((), ())), preferred_element_type=F32)


def before2(u):
    lane = lax.broadcasted_iota(jnp.int32, u.shape, 1)
    return jnp.where(
        lane < 64, jnp.where(lane % 32 != 0, pltpu.roll(u, 65, 1), 0.0), pltpu.roll(u, 64, 1)
    )


def after2(u):
    lane = lax.broadcasted_iota(jnp.int32, u.shape, 1)
    return jnp.where(
        lane >= 64, jnp.where(lane % 32 != 31, pltpu.roll(u, 63, 1), 0.0), pltpu.roll(u, 64, 1)
    )


def before(v):
    return jnp.concatenate([before2(v[:, 128:]), v[:, :128]], axis=1)


def after(v):
    return jnp.concatenate([v[:, 128:], after2(v[:, :128])], axis=1)


def kernel(
    gxn, gyn,
    inp, cot, w1t, w2t, b1r, b2r, depth_map, restore, pool_map, cot_map, toeplitz, gather, select, eye, place,
    out, gw1, gw2,
    xs, hb, hlr, hx, hc, w1, w1tr, w2, w2b, bias1, bias2, sl, gf, pool, cots, gs, gp,
    acc2, r2dp, s2a, r2gx, s2b, r2gy, gi, sby, ry, sx_, rx, sc, rc, acc1, s1, r1dp, s1a, r1gx, s1b, r1gy,
    ssem, rsem,
):
    gx, gy, dp = lax.axis_index("gx"), lax.axis_index("gy"), lax.axis_index("dp")

    def at(sx, sy):
        return (lax.rem(gx + sx + gxn, gxn), lax.rem(gy + sy + gyn, gyn), dp)

    def remote(src, dst, k, device):
        return pltpu.make_async_remote_copy(
            src_ref=src, dst_ref=dst, send_sem=ssem.at[k], recv_sem=rsem.at[k], device_id=device, device_id_type=MESH
        )

    barrier = pltpu.get_barrier_semaphore()
    peers = [at(*d) for d in DIRS]
    peers += [at(d, 0) for d in range(2, gxn - 1)] + [at(0, d) for d in range(2, gyn - 1)]
    peers += [(gx, gy, 1 - dp)]
    for peer in peers:
        pl.semaphore_signal(barrier, inc=1, device_id=peer, device_id_type=MESH)

    def raw(x):
        halves = [inp[n, :, x].reshape(64, 128) for n in range(2)]
        return jnp.concatenate(halves, axis=1)

    for x in range(8):
        hb[x] = dot(select[...], raw(x)).astype(BF16)
    pl.semaphore_wait(barrier, len(peers))
    first = []
    for k, (sx, sy) in enumerate(DIRS):
        a, b = (0 if sx == 1 else 1), (0 if sy == 1 else 1)
        if sx == 0:
            src, dst = hb, hlr.at[b]
        elif sy == 0:
            src, dst = inp.at[:, :, 7 if sx == 1 else 0], hx.at[a]
        else:
            src, dst = hb.at[7 if sx == 1 else 0], hc.at[a, b]
        first.append(remote(src, dst, k, at(sx, sy)))
        first[-1].start()

    small = dot_nt(eye[:32, :32], w1t[...]).astype(BF16)
    small = jnp.concatenate([small, jnp.zeros((32, 128 - 108), BF16)], axis=1)

    def fill(r, _):
        w1[pl.ds(pl.multiple_of(r * 32, 32), 32), :] = dot(small, toeplitz[r]).astype(BF16)
        return 0

    lax.fori_loop(0, 16, fill, 0)
    for b in range(6):
        width = min(128, 720 - b * 128)
        w1tr[b * 128:b * 128 + width] = dot_nt(eye[:width, :width], w1[:, b * 128:b * 128 + width]).astype(BF16)
    w2[...] = dot_nt(eye[:64, :64], w2t[...]).astype(BF16)
    for dx in range(3):
        for dy in range(3):
            at_lane = ((2 - dx) * 3 + 2 - dy) * 64
            row = (dx * 3 + dy) * 96
            w2b[:, at_lane:at_lane + 64] = w2t[row:row + 96, :]
    bias1[...] = jnp.zeros_like(bias1)
    bias1[:, 0:32] = jnp.broadcast_to(b1r[...], (128, 32))
    bias2[...] = jnp.zeros_like(bias2)
    bias2[:, 0:64] = jnp.broadcast_to(b2r[...], (128, 64))
    b1 = jnp.transpose(bias1[...])[:32]
    b2 = jnp.transpose(bias2[...])[:64]
    b1 = jnp.concatenate([b1, b1], axis=1)
    b2 = jnp.concatenate([b2, b2], axis=1)
    for q in range(4):
        part = jnp.concatenate(
            [cot[(n * 8 + h * 4 + q) * 32:(n * 8 + h * 4 + q) * 32 + 32, :] for n in range(2) for h in range(2)], axis=0
        )
        turned = dot_nt(eye[:64, :64], part).astype(BF16)
        cots[q * 64:q * 64 + 64] = dot(turned, cot_map[...]) * 0.125

    def slab(index, rows):
        spread = dot(rows, depth_map[...]).astype(BF16)
        for t in range(3):
            xs[index, t * 80:t * 80 + 64] = spread[:, t * 256:t * 256 + 256]

    for x in range(8):
        slab(x + 1, raw(x))
    acc2[...] = jnp.zeros_like(acc2)
    gi[...] = jnp.zeros_like(gi)
    acc1[...] = jnp.zeros_like(acc1)
    for copy in first:
        copy.wait()

    left, right = gy > 0, gy < gyn - 1
    up, down = gx > 0, gx < gxn - 1
    row16 = lax.broadcasted_iota(jnp.int32, (16, 256), 0)
    from_left = jnp.logical_and(row16 < 4, left)
    from_right = jnp.logical_and(jnp.logical_and(row16 >= 4, row16 < 8), right)

    def halo(index, left_rows, right_rows, ok):
        rows = jnp.where(from_left, left_rows.astype(F32), jnp.where(from_right, right_rows.astype(F32), 0.0))
        if ok is not None:
            rows = jnp.where(ok, rows, 0.0)
        spread = dot(rows.astype(BF16), depth_map[...]).astype(BF16)
        for t in range(3):
            xs[index, t * 80 + 64:t * 80 + 80] = spread[:, t * 256:t * 256 + 256]

    for x in range(8):
        halo(x + 1, hlr[0, x], hlr[1, x], None)
    for a, ok in ((0, up), (1, down)):
        index = 0 if a == 0 else 9
        rows = jnp.concatenate([hx[a, n].reshape(64, 128) for n in range(2)], axis=1)
        slab(index, jnp.where(ok, rows.astype(F32), 0.0).astype(BF16))
        halo(index, hc[a, 0], hc[a, 1], ok)

    b1all = jnp.concatenate([b1] * 16, axis=0)

    def layer1(j, _):
        total = None
        for px in range(2):
            x = 2 * j + px
            pre = dot(w1[...], xs[pl.ds(x, 3)].reshape(720, 256)) + b1all
            t = jnp.tanh(0.5 * pre)
            value = pre * (0.65 + 0.35 * t)
            sl[x] = 0.65 + 0.35 * t + 0.175 * pre * (1.0 - t * t)
            value = value[:256] + value[256:]
            value = value[:, :128] + value[:, 128:]
            total = value if total is None else total + value
        pool[j + 1, 1, 32:288] = (total * 0.125).astype(BF16)
        return 0

    lax.fori_loop(0, 4, layer1, 0)

    def exchange(ref, where, unit, base):
        copies = []
        for k, (sx, sy) in enumerate(DIRS):
            src_x, dst_x = {0: (pl.ds(1, 4),) * 2, 1: (4, 0), -1: (1, 5)}[sx]
            src_y, dst_y = {0: (pl.ds(unit, 8 * unit),) * 2, 1: (pl.ds(8 * unit, unit), pl.ds(0, unit)),
                            -1: (pl.ds(unit, unit), pl.ds(9 * unit, unit))}[sy]
            copies.append(
                remote(ref.at[(src_x,) + where + (src_y,)], ref.at[(dst_x,) + where + (dst_y,)], base + k, at(sx, sy))
            )
            copies[-1].start()
        return copies

    def clear(ref, where, unit):
        for ok, index in ((up, 0), (down, 5)):
            @pl.when(jnp.logical_not(ok))
            def _(index=index):
                ref[(index,) + where] = jnp.zeros((10 * unit, 128), BF16)
        for ok, index in ((left, 0), (right, 9 * unit)):
            @pl.when(jnp.logical_not(ok))
            def _(index=index):
                ref[(slice(None),) + where + (slice(index, index + unit),)] = jnp.zeros((6, unit, 128), BF16)

    for copy in exchange(pool, (1,), 32, 8):
        copy.wait()
    clear(pool, (1,), 32)
    for i in range(6):
        spread = dot(pool[i, 1], pool_map[...]).astype(BF16)
        pool[i, 0] = spread[:, :128]
        pool[i, 2] = spread[:, 128:]

    def cell(ref, i, where, start, size):
        rows = pl.ds(start, size)
        return jnp.concatenate([ref[(i,) + where + (rows,)], ref[(i + 2,) + where + (rows,)]], axis=1)

    for j in range(2):
        def layer2(y, _, j=j):
            patch = jnp.concatenate(
                [cell(pool, j + dx, (dz,), pl.multiple_of((y + dy) * 32, 32), 32)
                 for dx in range(3) for dy in range(3) for dz in range(3)], axis=0)
            pre = dot(w2[...], patch) + b2
            t = jnp.tanh(0.5 * pre)
            slope = 0.65 + 0.35 * t + 0.175 * pre * (1.0 - t * t)
            grad = (slope * cots[pl.ds(pl.multiple_of((y // 2) * 64, 64), 64), :]).astype(BF16)
            rows = pl.ds(pl.multiple_of((y + 1) * 64, 64), 64)
            gs[j + 1, rows] = grad[:, :128]
            gs[j + 3, rows] = grad[:, 128:]
            return 0

        lax.fori_loop(0, 8, layer2, 0)

    third = exchange(gs, (), 64, 16)

    for j in range(2):
        def weights2(y, _, j=j):
            grad = cell(gs, j + 1, (), pl.multiple_of((y + 1) * 64, 64), 64)
            for half in range(2):
                patch = jnp.concatenate(
                    [cell(pool, j + dx, (dz,), pl.multiple_of((y + dy) * 32 + half * 16, 16), 16)
                     for dx in range(3) for dy in range(3) for dz in range(3)], axis=0)
                acc2[half, :, 0:432] += dot_nt(grad, patch)
            return 0

        lax.fori_loop(0, 8, weights2, 0)
    pair2 = remote(acc2.at[1 - dp], r2dp, 24, (gx, gy, 1 - dp))
    pair2.start()
    for copy in third:
        copy.wait()
    clear(gs, (), 64)

    for j in range(2):
        def back2(y, _, j=j):
            patch = jnp.concatenate(
                [cell(gs, j + u, (), pl.multiple_of(y * 64, 64), 192) for u in range(3)], axis=0)
            terms = dot(w2b[...], patch) * 0.125
            rows = pl.ds(pl.multiple_of(y * 32, 32), 32)
            for h in range(2):
                part = terms[:, h * 128:h * 128 + 128]
                gp[j + 2 * h, rows] = part[32:64] + before2(part[64:96]) + after2(part[0:32])
            return 0

        lax.fori_loop(0, 8, back2, 0)

    pair2.wait()
    s2a[...] = (acc2[dp] + r2dp[...]).reshape(gxn, 8, 512)
    along2 = []
    for d in range(1, gxn):
        along2.append(remote(s2a.at[lax.rem(gx + d, gxn)], r2gx.at[d - 1], 24 + d, at(d, 0)))
        along2[-1].start()

    def back1(x, _):
        spread = gp[x // 2]
        spread = jnp.concatenate([spread, spread], axis=1)
        spread = jnp.concatenate([spread, spread], axis=0)
        grad = (sl[x] * spread).astype(BF16)
        gf[x] = grad
        gi[pl.ds(x, 3)] += dot(w1tr[...], grad).reshape(3, 240, 256)
        return 0

    lax.fori_loop(0, 8, back1, 0)

    def combine(x):
        return gi[x, 80:152] + before(gi[x, 160:232]) + after(gi[x, 0:72])

    for i, x in ((0, 0), (1, 9)):
        edge = combine(x)
        sx_[i] = edge[:64]
        sc[i] = edge[64:]

    def sum_terms(x, _):
        inner = combine(x + 1)
        gi[x + 1, 80:144] = inner[:64]
        sby[x] = inner[64:]
        return 0

    lax.fori_loop(0, 8, sum_terms, 0)
    fourth = []
    for k, (sx, sy) in enumerate(DIRS):
        a, b = (0 if sx == 1 else 1), (0 if sy == 1 else 1)
        if sx == 0:
            src, dst = sby, ry.at[b]
        elif sy == 0:
            src, dst = sx_.at[1 if sx == 1 else 0], rx.at[a]
        else:
            src, dst = sc.at[1 if sx == 1 else 0], rc.at[a, b]
        fourth.append(remote(src, dst, 40 + k, at(sx, sy)))
        fourth[-1].start()

    for copy in along2:
        copy.wait()
    total2 = s2a[gx]
    for d in range(1, gxn):
        total2 = total2 + r2gx[d - 1]
    for g in range(8):
        s2b[g] = total2[g:g + 1]
    across2 = []
    for d in range(1, gyn):
        across2.append(remote(s2b.at[lax.rem(gy + d, gyn)], r2gy.at[d - 1], 31 + d, at(0, d)))
        across2[-1].start()

    def weights1(x, _):
        acc1[...] += dot_nt(gf[x], xs[pl.ds(x, 3)].reshape(720, 256))
        return 0

    lax.fori_loop(0, 8, weights1, 0)
    taps = None
    for dy in range(3):
        kept = None
        for r in range(16):
            y = 2 * (r % 8) + r // 8
            term = jnp.where(place[...] == float(y + dy - 1), acc1[r * 32:r * 32 + 32], 0.0)
            kept = term if kept is None else kept + term
        high = kept.astype(BF16)
        rest = kept - high.astype(F32)
        mid = rest.astype(BF16)
        low = (rest - mid.astype(F32)).astype(BF16)
        parts = dot(jnp.concatenate([high, mid, low], axis=0), gather[dy])
        parts = parts[:32] + parts[32:64] + parts[64:]
        taps = parts if taps is None else taps + parts
    for g in range(8):
        s1[g] = taps[4 * g:4 * g + 4]
    pair1 = remote(s1, r1dp, 48, (gx, gy, 1 - dp))
    pair1.start()

    for copy in fourth:
        copy.wait()
    y16 = lax.broadcasted_iota(jnp.int32, (4, 16, 256), 1)

    def ends(low_rows, high_rows):
        low_part = jnp.where(jnp.logical_and(y16 == 0, left), low_rows[4:8][:, None, :], 0.0)
        high_part = jnp.where(jnp.logical_and(y16 == 15, right), high_rows[0:4][:, None, :], 0.0)
        return (low_part + high_part).reshape(64, 256)

    for a, ok, x in ((0, up, 1), (1, down, 8)):
        term = rx[a] + ends(rc[a, 0], rc[a, 1])
        gi[x, 80:144] += jnp.where(ok, term, 0.0)

    def finish(x, _):
        total = (gi[x + 1, 80:144] + ends(ry[0, x], ry[1, x])).astype(BF16)
        natural = dot(total, restore[...]).astype(BF16)
        for n in range(2):
            out[n, :, x] = natural[:, n * 128:n * 128 + 128].reshape(4, 16, 128)
        return 0

    lax.fori_loop(0, 8, finish, 0)

    pair1.wait()
    s1a[...] = s1[...] + r1dp[...]
    along1 = []
    for d in range(1, gxn):
        along1.append(remote(s1a.at[lax.rem(gx + d, gxn)], r1gx.at[d - 1], 48 + d, at(d, 0)))
        along1[-1].start()
    for copy in across2:
        copy.wait()
    total2 = s2b[gy]
    for d in range(1, gyn):
        total2 = total2 + r2gy[d - 1]
    gw2[...] = total2 * (1.0 / (CELLS / 8) ** 0.5)
    for copy in along1:
        copy.wait()
    total1 = s1a[gx]
    for d in range(1, gxn):
        total1 = total1 + r1gx[d - 1]
    s1b[...] = total1
    across1 = []
    for d in range(1, gyn):
        across1.append(remote(s1b, r1gy.at[d - 1], 55 + d, at(0, d)))
        across1[-1].start()
    for copy in across1:
        copy.wait()
    total1 = s1b[...]
    for d in range(1, gyn):
        total1 = total1 + r1gy[d - 1]
    mine = None
    for q in range(4):
        for c in range(4):
            ok = jnp.logical_and(gy // 2 == q, (gy % 2) * 2 + dp == c)
            term = jnp.where(ok, total1[q:q + 1, c * 32:c * 32 + 32], 0.0)
            mine = term if mine is None else mine + term
    gw1[:, 0:32] = mine * (1.0 / CELLS ** 0.5)


def on_device(gxn, gyn, consts, inputs, cotangent, w_first, w_second, b_first, b_second):
    cot = jnp.transpose(cotangent, (0, 2, 3, 4, 1)).reshape(512, 64)
    w1t = jnp.transpose(w_first, (2, 3, 4, 1, 0)).reshape(108, 32)
    w2t = jnp.transpose(w_second, (2, 3, 4, 1, 0)).reshape(864, 64)
    vmem = pl.BlockSpec(memory_space=pltpu.VMEM)
    operands = (inputs, cot, w1t, w2t, b_first.reshape(1, 32), b_second.reshape(1, 64), *consts)
    scratch = [
        ((10, 240, 256), BF16), ((8, 16, 256), BF16), ((2, 8, 16, 256), BF16), ((2, 2, 4, 16, 128), BF16),
        ((2, 2, 16, 256), BF16), ((512, 720), BF16), ((720, 512), BF16), ((64, 864), BF16), ((96, 576), BF16),
        ((128, 128), F32), ((128, 128), F32), ((8, 512, 256), F32), ((8, 512, 256), BF16), ((6, 3, 320, 128), BF16),
        ((256, 256), F32), ((6, 640, 128), BF16), ((4, 256, 128), F32),
        ((2, 64, 512), F32), ((64, 512), F32), ((gxn, 8, 512), F32), ((gxn - 1, 8, 512), F32), ((gyn, 1, 512), F32),
        ((gyn - 1, 1, 512), F32), ((10, 240, 256), F32), ((8, 8, 256), F32), ((2, 8, 8, 256), F32),
        ((2, 64, 256), F32), ((2, 64, 256), F32), ((2, 8, 256), F32), ((2, 2, 8, 256), F32), ((512, 720), F32),
        ((gxn, 4, 128), F32), ((gxn, 4, 128), F32), ((gxn, 4, 128), F32), ((gxn - 1, 4, 128), F32), ((4, 128), F32),
        ((gyn - 1, 4, 128), F32),
    ]
    result, part1, part2 = pl.pallas_call(
        functools.partial(kernel, gxn, gyn),
        out_shape=(
            jax.ShapeDtypeStruct(inputs.shape, BF16),
            jax.ShapeDtypeStruct((1, 128), F32),
            jax.ShapeDtypeStruct((1, 512), F32),
        ),
        in_specs=[vmem] * len(operands),
        out_specs=(vmem, vmem, vmem),
        scratch_shapes=[pltpu.VMEM(s, d) for s, d in scratch]
        + [pltpu.SemaphoreType.DMA((63,)), pltpu.SemaphoreType.DMA((63,))],
        compiler_params=pltpu.CompilerParams(
            collective_id=0, has_side_effects=True, vmem_limit_bytes=60 * 1024 * 1024
        ),
    )(*operands)
    grad_w2 = jnp.transpose(part2[0, :432].reshape(27, 16)).reshape(432)
    return result, part1[0, :27], grad_w2


def solution(mesh):
    consts = constants()
    return jax.shard_map(
        functools.partial(on_device, mesh.shape["gx"], mesh.shape["gy"], consts),
        mesh=mesh,
        in_specs=(P("dp", None, "gx", "gy", None), P("dp", None, "gx", "gy", None), P(), P(), P(), P()),
        out_specs=(P("dp", None, "gx", "gy", None), P(("gx", "gy", "dp")), P(("gx", "gy", "dp"))),
        check_vma=False,
    )
```

time: 999 us -> 72.7 us (0.07)
  matrix products: 440 us -> 0 us
  local copies, waits for them, and re-layouts: 206 us -> 5.7 us
  waiting for transfers between devices: 143 us -> 0 us
  other arithmetic: 139 us -> 0 us
  Pallas kernels: 0 us -> 66.1 us
  starting transfers between devices: 48.5 us -> 0 us
  between operations: 15.4 us -> 0.64 us
    conv_general_dilated x4 -> x0, matrix products: 336 us -> none  [conv_cells(): lax.conv_general_dilated(values, kernel, (1, 1, 1), [(margin, margin), (m...]
    unnamed x2 -> x0, waiting for transfers between devices: 125 us -> none
    transpose x2 -> x0, matrix products: 103 us -> none  [tap_grads(): return jnp.transpose(result, (1, 0, 2, 3, 4))]
    pallas_call x0 -> x1, Pallas kernels: none -> 66.1 us  [on_device(): pl.pallas_call(functools.partial(kernel, gxn, gyn), out_shape=(jax.ShapeD...]
    concatenate x7 -> x0, local copies, waits for them, and re-layouts: 57.1 us -> none  [extended(): x = jnp.concatenate([before, x, after], axis=dim)]
    concatenate x6 -> x0, other arithmetic: 53.4 us -> none  [the longest x5 52.6 us: extended(): x = jnp.concatenate([before, x, after], axis=dim)]
    ppermute x16 -> x0, starting transfers between devices: 48.5 us -> none  [the longest x8 37.9 us: extended(): before = lax.ppermute(last, axis, up)]
    conv_general_dilated x9 -> x0, local copies, waits for them, and re-layouts: 47.9 us -> none  [conv_cells(): lax.conv_general_dilated(values, kernel, (1, 1, 1), [(margin, margin), (m...]
  transfers between devices with their start and end apart: 17 -> 0, of which waited for: 7 -> 0; matrix products, arithmetic and copies ran while one was open for 22% -> 0% of each run, Pallas kernels for 0% -> 0%
where the time goes in v1:
time: 72.7 us; the launch traced here: 72.5 us
  Pallas kernels  66.1 us (91%)
  local copies, waits for them, and re-layouts  5.7 us (8%)
    pallas_call x1, Pallas kernels, on_device(): pl.pallas_call(functools.partial(kernel, gxn, gyn), out_shape=(jax.ShapeD...  66.1 us
    unnamed x1, local copies, waits for them, and re-layouts  1.67 us

profile of v1, /device:TPU:0, one launch (start us, length us, event | category | flops | bytes accessed | tf_op | source)
XLA Modules:
  0.0 72.5 jit_solution(8187529887915122032)
XLA Ops:
  0.6 1.4 %reshape.25.w1t = bf16[108,32]{1,0:T(8,128)(2,1)} reshape(bf16[3,3,3,4,32]{4,3,2,1,0:T(4,128)(2,1)} %bitcast.15) | data formatting | bytes 13824 | tf_op jit(solution)/shard_map/reshape | solution.py:459
  2.0 66.1 %shard_map.166 = (bf16[2,4,8,16,128]{4,3,2,1,0:T(8,128)(2,1)}, f32[1,128]{1,0:T(1,128)}, f32[1,512]{1,0:T(1,128)}) custom-call(bf16[2,4,8,16,128]{4,3,2,1,0:T(8,128)(2,1)} %inp.1, bf16[512,64]{1,0:T(8,128)(2,1)} %bitcast.13, bf16[108,32]{1,0:T(8,128)(2,1)} %reshape.25.w1t, bf16[864,64]{1,0:T(8,128)(2,1)} %bitcast.12, f32[1,32]{1,0:T(1,128)} %bitcast.16, ...), custom_call_target="tpu_custom_call" | custom-call | tf_op jit(solution)/shard_map/pallas_call | solution.py:474
  68.1 1.1 %slice_bitcast_fusion = f32[27]{0:T(128)} fusion(f32[1,128]{1,0:T(1,128)} %get-tuple-element.7), kind=kLoop, calls=%fused_computation.1 | loop fusion | bytes 216 | tf_op jit(solution)/shard_map/squeeze | solution.py:490
  69.3 0.7 slice_reduce_fusion
  70.0 0.1 reshape_squeeze.3
  70.0 0.1 copy.18
  70.1 0.7 reshape.29
  70.8 1.7 %copy.20 = bf16[2,4,8,16,128]{4,3,2,1,0:T(8,128)(2,1)} copy(bf16[2,4,8,16,128]{4,3,2,1,0:T(8,128)(2,1)} %get-tuple-element.12) | data formatting | bytes 524288

commit v2 on v1

--- a/solution.py
+++ b/solution.py
@@ -14,6 +14,7 @@
 BF16 = jnp.bfloat16
 DIRS = [(0, 1), (0, -1), (1, 0), (-1, 0), (1, 1), (1, -1), (-1, 1), (-1, -1)]
 CELLS = 4194304
+NCONST = 10
 
 
 def constants():
@@ -39,30 +40,29 @@
             for n in range(2):
                 for k in range(32):
                     cot_map[n * 64 + h * 32 + k, h * 128 + b * 64 + n * 32 + k] = 1
-    row_of = {}
     place = np.full((80,), -100.0, np.float32)
     chan = np.full((80,), -1)
     for c in range(4):
         for y in range(-1, 17):
             row = 64 + c if y < 0 else 68 + c if y > 15 else c * 16 + y
-            row_of[c, y] = row
             place[row] = y
             chan[row] = c
-    toeplitz = np.zeros((16, 128, 720), np.float32)
-    for r in range(16):
-        y = 2 * (r % 8) + r // 8
-        for dx in range(3):
-            for dy in range(3):
-                for dz in range(3):
-                    for c in range(4):
-                        tap = (dx * 3 + dy) * 3 + dz
-                        toeplitz[r, tap * 4 + c, dx * 240 + dz * 80 + row_of[c, y + dy - 1]] = 1
-    gather = np.zeros((3, 720, 128), np.float32)
-    for dy in range(3):
-        for dx in range(3):
-            for dz in range(3):
-                for row in range(72):
-                    gather[dy, dx * 240 + dz * 80 + row, chan[row] * 32 + dx * 9 + dy * 3 + dz] = 1
+    toeplitz = np.zeros((128, 3 * 768), np.float32)
+    gather = np.zeros((720, 128), np.float32)
+    for dx in range(3):
+        for dz in range(3):
+            group = dx * 240 + dz * 80
+            for c in range(4):
+                for dy in range(3):
+                    toeplitz[((dx * 3 + dy) * 3 + dz) * 4 + c, (group + c * 16 + dy - 1) % 768] = 1
+                toeplitz[((dx * 3 + 0) * 3 + dz) * 4 + c, 768 + group + 64 + c] = 1
+                toeplitz[((dx * 3 + 2) * 3 + dz) * 4 + c, 1536 + group + 68 + c] = 1
+            for row in range(72):
+                gather[group + row, chan[row] * 32 + dx * 9 + dz] = 1
+    reorder = np.zeros((432, 432), np.float32)
+    for tap in range(27):
+        for c in range(16):
+            reorder[tap * 16 + c, c * 27 + tap] = 1
     select = np.zeros((16, 64), np.float32)
     for c in range(4):
         select[c, c * 16 + 15] = 1
@@ -70,7 +70,7 @@
     b16 = lambda v: v.astype(ml_dtypes.bfloat16)
     return (
         b16(depth_map), b16(restore), b16(pool_map), b16(cot_map), b16(toeplitz), b16(gather), b16(select),
-        b16(np.eye(128, dtype=np.float32)), np.tile(place, 9)[None, :],
+        b16(np.eye(128, dtype=np.float32)), b16(reorder), np.pad(np.tile(place, 9), (0, 48), constant_values=-100)[None, :],
     )
 
 
@@ -80,6 +80,16 @@
 
 def dot_nt(a, b):
     return lax.dot_general(a, b, (((1,), (1,)), ((), ())), preferred_element_type=F32)
+
+
+def split_dot(a, b):
+    high = a.astype(BF16)
+    rest = a - high.astype(F32)
+    mid = rest.astype(BF16)
+    low = (rest - mid.astype(F32)).astype(BF16)
+    parts = dot(jnp.concatenate([high.astype(F32), mid.astype(F32), low.astype(F32)], axis=0).astype(BF16), b)
+    rows = a.shape[0]
+    return parts[:rows] + parts[rows:2 * rows] + parts[2 * rows:]
 
 
 def before2(u):
@@ -106,12 +116,17 @@
 
 def kernel(
     gxn, gyn,
-    inp, cot, w1t, w2t, b1r, b2r, depth_map, restore, pool_map, cot_map, toeplitz, gather, select, eye, place,
-    out, gw1, gw2,
-    xs, hb, hlr, hx, hc, w1, w1tr, w2, w2b, bias1, bias2, sl, gf, pool, cots, gs, gp,
+    inp, cot, w1t, w2t, b1r, b2r, *rest):
+    fixed, rest = rest[:NCONST], rest[NCONST:]
+    out, gw1, gw2 = rest[:3]
+    kept, rest = rest[3:3 + NCONST], rest[3 + NCONST:]
+    (xs, hb, hlr, hx, hc, w1, w1tr, w2, w2b, bias1, bias2, sl, gf, pool, cots, gs, gp,
     acc2, r2dp, s2a, r2gx, s2b, r2gy, gi, sby, ry, sx_, rx, sc, rc, acc1, s1, r1dp, s1a, r1gx, s1b, r1gy,
-    ssem, rsem,
-):
+    w1f, ssem, rsem, lsem) = rest
+    depth_map, restore, pool_map, cot_map, toeplitz, gather, select, eye, reorder, place = kept
+    loads = [pltpu.make_async_copy(fixed[i], kept[i], lsem.at[i]) for i in range(NCONST)]
+    for load in loads:
+        load.start()
     gx, gy, dp = lax.axis_index("gx"), lax.axis_index("gy"), lax.axis_index("dp")
 
     def at(sx, sy):
@@ -133,6 +148,7 @@
         halves = [inp[n, :, x].reshape(64, 128) for n in range(2)]
         return jnp.concatenate(halves, axis=1)
 
+    loads[6].wait()
     for x in range(8):
         hb[x] = dot(select[...], raw(x)).astype(BF16)
     pl.semaphore_wait(barrier, len(peers))
@@ -148,14 +164,23 @@
         first.append(remote(src, dst, k, at(sx, sy)))
         first[-1].start()
 
-    small = dot_nt(eye[:32, :32], w1t[...]).astype(BF16)
-    small = jnp.concatenate([small, jnp.zeros((32, 128 - 108), BF16)], axis=1)
-
-    def fill(r, _):
-        w1[pl.ds(pl.multiple_of(r * 32, 32), 32), :] = dot(small, toeplitz[r]).astype(BF16)
-        return 0
-
-    lax.fori_loop(0, 16, fill, 0)
+    for i, load in enumerate(loads):
+        if i != 6:
+            load.wait()
+    w1f[...] = jnp.zeros_like(w1f)
+    for tap in range(27):
+        w1f[tap * 4:tap * 4 + 4] = w1t[tap].astype(F32)
+    small = dot_nt(eye[:32, :32], w1f[...].astype(BF16)).astype(BF16)
+    base = dot(small, toeplitz[...])
+    for r in range(16):
+        y = 2 * (r % 8) + r // 8
+        block = base[:, :768] if y == 0 else pltpu.roll(base[:, :768], y, 1)
+        block = jnp.where(jnp.abs(place[...] - float(y)) < 1.5, block, 0.0)
+        if y == 0:
+            block = block + base[:, 768:1536]
+        if y == 15:
+            block = block + base[:, 1536:]
+        w1[r * 32:r * 32 + 32, :] = block[:, :720].astype(BF16)
     for b in range(6):
         width = min(128, 720 - b * 128)
         w1tr[b * 128:b * 128 + width] = dot_nt(eye[:width, :width], w1[:, b * 128:b * 128 + width]).astype(BF16)
@@ -188,8 +213,6 @@
     for x in range(8):
         slab(x + 1, raw(x))
     acc2[...] = jnp.zeros_like(acc2)
-    gi[...] = jnp.zeros_like(gi)
-    acc1[...] = jnp.zeros_like(acc1)
     for copy in first:
         copy.wait()
 
@@ -231,7 +254,7 @@
         pool[j + 1, 1, 32:288] = (total * 0.125).astype(BF16)
         return 0
 
-    lax.fori_loop(0, 4, layer1, 0)
+    lax.fori_loop(0, 4, layer1, 0, unroll=True)
 
     def exchange(ref, where, unit, base):
         copies = []
@@ -281,7 +304,7 @@
             gs[j + 3, rows] = grad[:, 128:]
             return 0
 
-        lax.fori_loop(0, 8, layer2, 0)
+        lax.fori_loop(0, 8, layer2, 0, unroll=True)
 
     third = exchange(gs, (), 64, 16)
 
@@ -295,7 +318,7 @@
                 acc2[half, :, 0:432] += dot_nt(grad, patch)
             return 0
 
-        lax.fori_loop(0, 8, weights2, 0)
+        lax.fori_loop(0, 8, weights2, 0, unroll=True)
     pair2 = remote(acc2.at[1 - dp], r2dp, 24, (gx, gy, 1 - dp))
     pair2.start()
     for copy in third:
@@ -313,7 +336,7 @@
                 gp[j + 2 * h, rows] = part[32:64] + before2(part[64:96]) + after2(part[0:32])
             return 0
 
-        lax.fori_loop(0, 8, back2, 0)
+        lax.fori_loop(0, 8, back2, 0, unroll=True)
 
     pair2.wait()
     s2a[...] = (acc2[dp] + r2dp[...]).reshape(gxn, 8, 512)
@@ -322,16 +345,56 @@
         along2.append(remote(s2a.at[lax.rem(gx + d, gxn)], r2gx.at[d - 1], 24 + d, at(d, 0)))
         along2[-1].start()
 
-    def back1(x, _):
+    for x in range(8):
         spread = gp[x // 2]
         spread = jnp.concatenate([spread, spread], axis=1)
         spread = jnp.concatenate([spread, spread], axis=0)
-        grad = (sl[x] * spread).astype(BF16)
-        gf[x] = grad
-        gi[pl.ds(x, 3)] += dot(w1tr[...], grad).reshape(3, 240, 256)
-        return 0
-
-    lax.fori_loop(0, 8, back1, 0)
+        gf[x] = (sl[x] * spread).astype(BF16)
+    for x in range(8):
+        term = dot_nt(gf[x], xs[x:x + 3].reshape(720, 256))
+        acc1[...] = term if x == 0 else acc1[...] + term
+
+    taps = None
+    for dy in range(3):
+        kept = None
+        for r in range(16):
+            y = 2 * (r % 8) + r // 8
+            term = jnp.where(place[:, :720] == float(y + dy - 1), acc1[r * 32:r * 32 + 32], 0.0)
+            kept = term if kept is None else kept + term
+        parts = split_dot(kept, gather[...])
+        if dy:
+            parts = pltpu.roll(parts, 3 * dy, 1)
+        taps = parts if taps is None else taps + parts
+    for g in range(8):
+        s1[g] = taps[4 * g:4 * g + 4]
+    pair1 = remote(s1, r1dp, 48, (gx, gy, 1 - dp))
+    pair1.start()
+    for copy in along2:
+        copy.wait()
+    total2 = s2a[gx]
+    for d in range(1, gxn):
+        total2 = total2 + r2gx[d - 1]
+    for g in range(8):
+        s2b[g] = total2[g:g + 1]
+    across2 = []
+    for d in range(1, gyn):
+        across2.append(remote(s2b.at[lax.rem(gy + d, gyn)], r2gy.at[d - 1], 31 + d, at(0, d)))
+        across2[-1].start()
+
+    for x in range(8):
+        term = dot(w1tr[...], gf[x]).reshape(3, 240, 256)
+        if x == 0:
+            gi[0:3] = term
+        else:
+            gi[x:x + 2] += term[:2]
+            gi[x + 2] = term[2]
+        if x == 3:
+            pair1.wait()
+            s1a[...] = s1[...] + r1dp[...]
+            along1 = []
+            for d in range(1, gxn):
+                along1.append(remote(s1a.at[lax.rem(gx + d, gxn)], r1gx.at[d - 1], 48 + d, at(d, 0)))
+                along1[-1].start()
 
     def combine(x):
         return gi[x, 80:152] + before(gi[x, 160:232]) + after(gi[x, 0:72])
@@ -340,14 +403,10 @@
         edge = combine(x)
         sx_[i] = edge[:64]
         sc[i] = edge[64:]
-
-    def sum_terms(x, _):
+    for x in range(8):
         inner = combine(x + 1)
         gi[x + 1, 80:144] = inner[:64]
         sby[x] = inner[64:]
-        return 0
-
-    lax.fori_loop(0, 8, sum_terms, 0)
     fourth = []
     for k, (sx, sy) in enumerate(DIRS):
         a, b = (0 if sx == 1 else 1), (0 if sy == 1 else 1)
@@ -359,77 +418,6 @@
             src, dst = sc.at[1 if sx == 1 else 0], rc.at[a, b]
         fourth.append(remote(src, dst, 40 + k, at(sx, sy)))
         fourth[-1].start()
-
-    for copy in along2:
-        copy.wait()
-    total2 = s2a[gx]
-    for d in range(1, gxn):
-        total2 = total2 + r2gx[d - 1]
-    for g in range(8):
-        s2b[g] = total2[g:g + 1]
-    across2 = []
-    for d in range(1, gyn):
-        across2.append(remote(s2b.at[lax.rem(gy + d, gyn)], r2gy.at[d - 1], 31 + d, at(0, d)))
-        across2[-1].start()
-
-    def weights1(x, _):
-        acc1[...] += dot_nt(gf[x], xs[pl.ds(x, 3)].reshape(720, 256))
-        return 0
-
-    lax.fori_loop(0, 8, weights1, 0)
-    taps = None
-    for dy in range(3):
-        kept = None
-        for r in range(16):
-            y = 2 * (r % 8) + r // 8
-            term = jnp.where(place[...] == float(y + dy - 1), acc1[r * 32:r * 32 + 32], 0.0)
-            kept = term if kept is None else kept + term
-        high = kept.astype(BF16)
-        rest = kept - high.astype(F32)
-        mid = rest.astype(BF16)
-        low = (rest - mid.astype(F32)).astype(BF16)
-        parts = dot(jnp.concatenate([high, mid, low], axis=0), gather[dy])
-        parts = parts[:32] + parts[32:64] + parts[64:]
-        taps = parts if taps is None else taps + parts
-    for g in range(8):
-        s1[g] = taps[4 * g:4 * g + 4]
-    pair1 = remote(s1, r1dp, 48, (gx, gy, 1 - dp))
-    pair1.start()
-
-    for copy in fourth:
-        copy.wait()
-    y16 = lax.broadcasted_iota(jnp.int32, (4, 16, 256), 1)
-
-    def ends(low_rows, high_rows):
-        low_part = jnp.where(jnp.logical_and(y16 == 0, left), low_rows[4:8][:, None, :], 0.0)
-        high_part = jnp.where(jnp.logical_and(y16 == 15, right), high_rows[0:4][:, None, :], 0.0)
-        return (low_part + high_part).reshape(64, 256)
-
-    for a, ok, x in ((0, up, 1), (1, down, 8)):
-        term = rx[a] + ends(rc[a, 0], rc[a, 1])
-        gi[x, 80:144] += jnp.where(ok, term, 0.0)
-
-    def finish(x, _):
-        total = (gi[x + 1, 80:144] + ends(ry[0, x], ry[1, x])).astype(BF16)
-        natural = dot(total, restore[...]).astype(BF16)
-        for n in range(2):
-            out[n, :, x] = natural[:, n * 128:n * 128 + 128].reshape(4, 16, 128)
-        return 0
-
-    lax.fori_loop(0, 8, finish, 0)
-
-    pair1.wait()
-    s1a[...] = s1[...] + r1dp[...]
-    along1 = []
-    for d in range(1, gxn):
-        along1.append(remote(s1a.at[lax.rem(gx + d, gxn)], r1gx.at[d - 1], 48 + d, at(d, 0)))
-        along1[-1].start()
-    for copy in across2:
-        copy.wait()
-    total2 = s2b[gy]
-    for d in range(1, gyn):
-        total2 = total2 + r2gy[d - 1]
-    gw2[...] = total2 * (1.0 / (CELLS / 8) ** 0.5)
     for copy in along1:
         copy.wait()
     total1 = s1a[gx]
@@ -440,6 +428,36 @@
     for d in range(1, gyn):
         across1.append(remote(s1b, r1gy.at[d - 1], 55 + d, at(0, d)))
         across1[-1].start()
+    for copy in across2:
+        copy.wait()
+    total2 = s2b[gy]
+    for d in range(1, gyn):
+        total2 = total2 + r2gy[d - 1]
+    total2 = jnp.concatenate([total2 * (1.0 / (CELLS / 8) ** 0.5)] * 8, axis=0)[:, :432]
+    gw2[...] = split_dot(total2, reorder[...])[0:1]
+
+    for copy in fourth:
+        copy.wait()
+    y16 = lax.broadcasted_iota(jnp.int32, (4, 16, 256), 1)
+
+    def ends(low_rows, high_rows):
+        low_part = jnp.where(jnp.logical_and(y16 == 0, left), low_rows[4:8][:, None, :], 0.0)
+        high_part = jnp.where(jnp.logical_and(y16 == 15, right), high_rows[0:4][:, None, :], 0.0)
+        return (low_part + high_part).reshape(64, 256)
+
+    for a, ok, x in ((0, up, 1), (1, down, 8)):
+        term = rx[a] + ends(rc[a, 0], rc[a, 1])
+        gi[x, 80:144] += jnp.where(ok, term, 0.0)
+
+    def finish(x, _):
+        total = (gi[x + 1, 80:144] + ends(ry[0, x], ry[1, x])).astype(BF16)
+        natural = dot(total, restore[...]).astype(BF16)
+        for n in range(2):
+            out[n, :, x] = natural[:, n * 128:n * 128 + 128].reshape(4, 16, 128)
+        return 0
+
+    lax.fori_loop(0, 8, finish, 0, unroll=True)
+
     for copy in across1:
         copy.wait()
     total1 = s1b[...]
@@ -451,12 +469,12 @@
             ok = jnp.logical_and(gy // 2 == q, (gy % 2) * 2 + dp == c)
             term = jnp.where(ok, total1[q:q + 1, c * 32:c * 32 + 32], 0.0)
             mine = term if mine is None else mine + term
-    gw1[:, 0:32] = mine * (1.0 / CELLS ** 0.5)
+    gw1[...] = mine[:, 0:27] * (1.0 / CELLS ** 0.5)
 
 
 def on_device(gxn, gyn, consts, inputs, cotangent, w_first, w_second, b_first, b_second):
     cot = jnp.transpose(cotangent, (0, 2, 3, 4, 1)).reshape(512, 64)
-    w1t = jnp.transpose(w_first, (2, 3, 4, 1, 0)).reshape(108, 32)
+    w1t = jnp.transpose(w_first, (2, 3, 4, 1, 0)).reshape(27, 4, 32)
     w2t = jnp.transpose(w_second, (2, 3, 4, 1, 0)).reshape(864, 64)
     vmem = pl.BlockSpec(memory_space=pltpu.VMEM)
     operands = (inputs, cot, w1t, w2t, b_first.reshape(1, 32), b_second.reshape(1, 64), *consts)
@@ -469,25 +487,25 @@
         ((gyn - 1, 1, 512), F32), ((10, 240, 256), F32), ((8, 8, 256), F32), ((2, 8, 8, 256), F32),
         ((2, 64, 256), F32), ((2, 64, 256), F32), ((2, 8, 256), F32), ((2, 2, 8, 256), F32), ((512, 720), F32),
         ((gxn, 4, 128), F32), ((gxn, 4, 128), F32), ((gxn, 4, 128), F32), ((gxn - 1, 4, 128), F32), ((4, 128), F32),
-        ((gyn - 1, 4, 128), F32),
+        ((gyn - 1, 4, 128), F32), ((128, 32), F32),
     ]
     result, part1, part2 = pl.pallas_call(
         functools.partial(kernel, gxn, gyn),
         out_shape=(
             jax.ShapeDtypeStruct(inputs.shape, BF16),
-            jax.ShapeDtypeStruct((1, 128), F32),
-            jax.ShapeDtypeStruct((1, 512), F32),
+            jax.ShapeDtypeStruct((1, 27), F32),
+            jax.ShapeDtypeStruct((1, 432), F32),
         ),
-        in_specs=[vmem] * len(operands),
+        in_specs=[vmem] * 6 + [pl.BlockSpec(memory_space=pl.ANY)] * NCONST,
         out_specs=(vmem, vmem, vmem),
-        scratch_shapes=[pltpu.VMEM(s, d) for s, d in scratch]
-        + [pltpu.SemaphoreType.DMA((63,)), pltpu.SemaphoreType.DMA((63,))],
+        scratch_shapes=[pltpu.VMEM(c.shape, c.dtype) for c in consts]
+        + [pltpu.VMEM(s, d) for s, d in scratch]
+        + [pltpu.SemaphoreType.DMA((63,)), pltpu.SemaphoreType.DMA((63,)), pltpu.SemaphoreType.DMA((NCONST,))],
         compiler_params=pltpu.CompilerParams(
             collective_id=0, has_side_effects=True, vmem_limit_bytes=60 * 1024 * 1024
         ),
     )(*operands)
-    grad_w2 = jnp.transpose(part2[0, :432].reshape(27, 16)).reshape(432)
-    return result, part1[0, :27], grad_w2
+    return result, part1.reshape(27), part2.reshape(432)
 
 
 def solution(mesh):

time: 72.7 us -> 57.1 us (0.79)
  Pallas kernels: 66.1 us -> 53.5 us
  local copies, waits for them, and re-layouts: 5.7 us -> 2.77 us
    pallas_call x1, Pallas kernels: 66.1 us -> 53.5 us  [on_device(): pl.pallas_call(functools.partial(kernel, gxn, gyn), out_shape=(jax.ShapeD...]
    reshape x2 -> x0, local copies, waits for them, and re-layouts: 2.05 us -> none  [the longest x1 1.38 us: on_device(): w1t = jnp.transpose(w_first, (2, 3, 4, 1, 0)).reshape(108, 32)]
    squeeze x1 -> x0, local copies, waits for them, and re-layouts: 1.13 us -> none  [on_device(): return (result, part1[0, :27], grad_w2)]
    unnamed x1 -> x7, local copies, waits for them, and re-layouts: 1.67 us -> 2.77 us
where the time goes in v2:
time: 57.1 us; the launch traced here: 56.9 us
  Pallas kernels  53.5 us (94%)
  local copies, waits for them, and re-layouts  2.77 us (5%)
  between operations  0.66 us (1%)
    pallas_call x1, Pallas kernels, on_device(): pl.pallas_call(functools.partial(kernel, gxn, gyn), out_shape=(jax.ShapeD...  53.5 us
    unnamed x7, local copies, waits for them, and re-layouts  2.77 us

profile of v2, /device:TPU:0, one launch (start us, length us, event | category | flops | bytes accessed | tf_op | source)
XLA Modules:
  0.0 56.9 jit_solution(14459159826655866570)
XLA Ops:
  0.6 53.5 %shard_map.175 = (bf16[2,4,8,16,128]{4,3,2,1,0:T(8,128)(2,1)}, f32[1,27]{1,0:T(1,128)}, f32[1,432]{1,0:T(1,128)}) custom-call(bf16[2,4,8,16,128]{4,3,2,1,0:T(8,128)(2,1)} %inp.1, bf16[512,64]{1,0:T(8,128)(2,1)} %bitcast.14, bf16[27,4,32]{2,1,0:T(4,128)(2,1)} %bitcast.15, bf16[864,64]{1,0:T(8,128)(2,1)} %bitcast.13, f32[1,32]{1,0:T(1,128)} %bitcast.17, ...), custom_call_target="tpu_custom_call" | custom-call | tf_op jit(solution)/shard_map/pallas_call | solution.py:492
  54.1 0.0 copy-start.1
  54.1 0.0 copy-start
  54.1 1.7 %copy.22 = bf16[2,4,8,16,128]{4,3,2,1,0:T(8,128)(2,1)} copy(bf16[2,4,8,16,128]{4,3,2,1,0:T(8,128)(2,1)} %get-tuple-element.12) | data formatting | bytes 524288
  55.8 0.0 copy-done.1
  55.8 0.5 copy.23
  56.3 0.0 copy-done
  56.3 0.6 %copy.24 = f32[432]{0:T(512)} copy(f32[432]{0:T(512)S(1)} %bitcast.16) | data formatting | bytes 3456
Async XLA Ops:
  54.1 1.7 %copy-start.1 = (f32[1,27]{1,0:T(1,128)S(1)}, f32[1,27]{1,0:T(1,128)}, u32[]{:S(2)}) copy-start(f32[1,27]{1,0:T(1,128)} %get-tuple-element.7) | copy-start | bytes 328
  54.1 2.2 %copy-start = (f32[1,432]{1,0:T(1,128)S(1)}, f32[1,432]{1,0:T(1,128)}, u32[]{:S(2)}) copy-start(f32[1,432]{1,0:T(1,128)} %get-tuple-element.8) | copy-start | bytes 5188

commit v3 on v2

--- a/solution.py
+++ b/solution.py
@@ -121,8 +121,8 @@
     out, gw1, gw2 = rest[:3]
     kept, rest = rest[3:3 + NCONST], rest[3 + NCONST:]
     (xs, hb, hlr, hx, hc, w1, w1tr, w2, w2b, bias1, bias2, sl, gf, pool, cots, gs, gp,
-    acc2, r2dp, s2a, r2gx, s2b, r2gy, gi, sby, ry, sx_, rx, sc, rc, acc1, s1, r1dp, s1a, r1gx, s1b, r1gy,
-    w1f, ssem, rsem, lsem) = rest
+    acc2, r2dp, s2a, r2gx, s2b, r2gy, gi, sby, ry, sx_, rx, sc, rc, acc1, s1, r1gx, s1b, r1gy,
+    w1f, w2e, pre2, xe, ye, rxe, rye, rce, ssem, rsem, lsem) = rest
     depth_map, restore, pool_map, cot_map, toeplitz, gather, select, eye, reorder, place = kept
     loads = [pltpu.make_async_copy(fixed[i], kept[i], lsem.at[i]) for i in range(NCONST)]
     for load in loads:
@@ -137,10 +137,37 @@
             src_ref=src, dst_ref=dst, send_sem=ssem.at[k], recv_sem=rsem.at[k], device_id=device, device_id_type=MESH
         )
 
+    left, right = gy > 0, gy < gyn - 1
+    up, down = gx > 0, gx < gxn - 1
+
+    def start(copies, which):
+        for sx in which:
+            picked = [c for c, d in zip(copies, DIRS) if d[0] == sx]
+            if sx == 0:
+                for copy in picked:
+                    copy.start()
+            else:
+                @pl.when(down if sx == 1 else up)
+                def _(picked=picked):
+                    for copy in picked:
+                        copy.start()
+
+    def finish_all(copies):
+        by = {sx: [c for c, d in zip(copies, DIRS) if d[0] == sx] for sx in (0, 1, -1)}
+        for sx in (1, -1):
+            @pl.when(down if sx == 1 else up)
+            def _(sx=sx):
+                for copy in by[sx]:
+                    copy.wait_send()
+                for copy in by[-sx]:
+                    copy.wait_recv()
+        for copy in by[0]:
+            copy.wait()
+
     barrier = pltpu.get_barrier_semaphore()
     peers = [at(*d) for d in DIRS]
     peers += [at(d, 0) for d in range(2, gxn - 1)] + [at(0, d) for d in range(2, gyn - 1)]
-    peers += [(gx, gy, 1 - dp)]
+    peers += [(lax.rem(gx + d, gxn), gy, 1 - dp) for d in range(gxn)]
     for peer in peers:
         pl.semaphore_signal(barrier, inc=1, device_id=peer, device_id_type=MESH)
 
@@ -162,7 +189,7 @@
         else:
             src, dst = hb.at[7 if sx == 1 else 0], hc.at[a, b]
         first.append(remote(src, dst, k, at(sx, sy)))
-        first[-1].start()
+    start(first, (1, -1, 0))
 
     for i, load in enumerate(loads):
         if i != 6:
@@ -213,11 +240,17 @@
     for x in range(8):
         slab(x + 1, raw(x))
     acc2[...] = jnp.zeros_like(acc2)
-    for copy in first:
-        copy.wait()
-
-    left, right = gy > 0, gy < gyn - 1
-    up, down = gx > 0, gx < gxn - 1
+    for i in (0, 5):
+        gs[i] = jnp.zeros((768, 128), BF16)
+    for i in range(1, 5):
+        gs[i, 0:128] = jnp.zeros((128, 128), BF16)
+        gs[i, 640:768] = jnp.zeros((128, 128), BF16)
+    for i, picked in enumerate((
+        [(0, dy) for dy in range(3)], [(2, dy) for dy in range(3)], [(dx, 0) for dx in range(3)], [(dx, 2) for dx in range(3)]
+    )):
+        rows = [w2t[(dx * 3 + dy) * 96:(dx * 3 + dy) * 96 + 96, :] for dx, dy in picked]
+        w2e[i] = dot_nt(eye[:64, :64], jnp.concatenate(rows, axis=0)).astype(BF16)
+    finish_all(first)
     row16 = lax.broadcasted_iota(jnp.int32, (16, 256), 0)
     from_left = jnp.logical_and(row16 < 4, left)
     from_right = jnp.logical_and(jnp.logical_and(row16 >= 4, row16 < 8), right)
@@ -240,11 +273,11 @@
 
     b1all = jnp.concatenate([b1] * 16, axis=0)
 
-    def layer1(j, _):
+    def layer1(j):
         total = None
         for px in range(2):
             x = 2 * j + px
-            pre = dot(w1[...], xs[pl.ds(x, 3)].reshape(720, 256)) + b1all
+            pre = dot(w1[...], xs[x:x + 3].reshape(720, 256)) + b1all
             t = jnp.tanh(0.5 * pre)
             value = pre * (0.65 + 0.35 * t)
             sl[x] = 0.65 + 0.35 * t + 0.175 * pre * (1.0 - t * t)
@@ -252,98 +285,142 @@
             value = value[:, :128] + value[:, 128:]
             total = value if total is None else total + value
         pool[j + 1, 1, 32:288] = (total * 0.125).astype(BF16)
-        return 0
-
-    lax.fori_loop(0, 4, layer1, 0, unroll=True)
-
-    def exchange(ref, where, unit, base):
-        copies = []
-        for k, (sx, sy) in enumerate(DIRS):
-            src_x, dst_x = {0: (pl.ds(1, 4),) * 2, 1: (4, 0), -1: (1, 5)}[sx]
-            src_y, dst_y = {0: (pl.ds(unit, 8 * unit),) * 2, 1: (pl.ds(8 * unit, unit), pl.ds(0, unit)),
-                            -1: (pl.ds(unit, unit), pl.ds(9 * unit, unit))}[sy]
-            copies.append(
-                remote(ref.at[(src_x,) + where + (src_y,)], ref.at[(dst_x,) + where + (dst_y,)], base + k, at(sx, sy))
-            )
-            copies[-1].start()
-        return copies
-
-    def clear(ref, where, unit):
-        for ok, index in ((up, 0), (down, 5)):
-            @pl.when(jnp.logical_not(ok))
-            def _(index=index):
-                ref[(index,) + where] = jnp.zeros((10 * unit, 128), BF16)
-        for ok, index in ((left, 0), (right, 9 * unit)):
-            @pl.when(jnp.logical_not(ok))
-            def _(index=index):
-                ref[(slice(None),) + where + (slice(index, index + unit),)] = jnp.zeros((6, unit, 128), BF16)
-
-    for copy in exchange(pool, (1,), 32, 8):
-        copy.wait()
-    clear(pool, (1,), 32)
-    for i in range(6):
+
+    second = []
+    for k, (sx, sy) in enumerate(DIRS):
+        src_x, dst_x = {0: (pl.ds(1, 4),) * 2, 1: (4, 0), -1: (1, 5)}[sx]
+        src_y, dst_y = {0: (pl.ds(32, 256),) * 2, 1: (pl.ds(256, 32), pl.ds(0, 32)), -1: (pl.ds(32, 32), pl.ds(288, 32))}[sy]
+        second.append(remote(pool.at[src_x, 1, src_y], pool.at[dst_x, 1, dst_y], 8 + k, at(sx, sy)))
+    layer1(0)
+    layer1(3)
+    start(second, (1, -1))
+    layer1(1)
+    layer1(2)
+    start(second, (0,))
+
+    for i in range(1, 5):
+        spread = dot(pool[i, 1, 32:288], pool_map[...]).astype(BF16)
+        pool[i, 0, 32:288] = spread[:, :128]
+        pool[i, 2, 32:288] = spread[:, 128:]
+    none = jnp.zeros((32, 128), BF16)
+
+    def piece(i, dz, r):
+        return none if i in (0, 5) or r in (0, 9) else pool[i, dz, r * 32:r * 32 + 32]
+
+    def pair(i, dz, r):
+        return jnp.concatenate([piece(i, dz, r), piece(i + 2, dz, r)], axis=1)
+
+    for j in range(2):
+        for y in range(8):
+            patch = jnp.concatenate(
+                [pair(j + dx, dz, y + dy) for dx in range(3) for dy in range(3) for dz in range(3)], axis=0)
+            pre2[j, y] = dot(w2[...], patch) + b2
+
+    finish_all(second)
+    for ok, index in ((up, 0), (down, 5)):
+        @pl.when(jnp.logical_not(ok))
+        def _(index=index):
+            pool[index, 1] = jnp.zeros((320, 128), BF16)
+    for ok, index in ((left, 0), (right, 288)):
+        @pl.when(jnp.logical_not(ok))
+        def _(index=index):
+            pool[:, 1, index:index + 32] = jnp.zeros((6, 32, 128), BF16)
+
+    for i in (0, 5):
         spread = dot(pool[i, 1], pool_map[...]).astype(BF16)
         pool[i, 0] = spread[:, :128]
         pool[i, 2] = spread[:, 128:]
-
-    def cell(ref, i, where, start, size):
-        rows = pl.ds(start, size)
-        return jnp.concatenate([ref[(i,) + where + (rows,)], ref[(i + 2,) + where + (rows,)]], axis=1)
-
+    rims = [(i, r) for i in range(1, 5) for r in (0, 288)]
+    spread = dot(jnp.concatenate([pool[i, 1, r:r + 32] for i, r in rims], axis=0), pool_map[...]).astype(BF16)
+    for q, (i, r) in enumerate(rims):
+        pool[i, 0, r:r + 32] = spread[q * 32:q * 32 + 32, :128]
+        pool[i, 2, r:r + 32] = spread[q * 32:q * 32 + 32, 128:]
+    for side, i in ((0, 0), (1, 5)):
+        for y in range(4):
+            patch = jnp.concatenate(
+                [jnp.concatenate([pool[i, dz, (q + dy) * 32:(q + dy) * 32 + 32] for q in (y, y + 4)], axis=1)
+                 for dy in range(3) for dz in range(3)], axis=0)
+            term = dot(w2e[side], patch)
+            lanes = slice(side * 128, side * 128 + 128)
+            pre2[side, y, :, lanes] += term[:, :128]
+            pre2[side, y + 4, :, lanes] += term[:, 128:]
+    for side, y, r in ((2, 0, 0), (3, 7, 288)):
+        for j in range(2):
+            patch = jnp.concatenate(
+                [jnp.concatenate([none if i in (0, 5) else pool[i, dz, r:r + 32] for i in (j + dx, j + dx + 2)], axis=1)
+                 for dx in range(3) for dz in range(3)], axis=0)
+            pre2[j, y] += dot(w2e[side], patch)
     for j in range(2):
-        def layer2(y, _, j=j):
-            patch = jnp.concatenate(
-                [cell(pool, j + dx, (dz,), pl.multiple_of((y + dy) * 32, 32), 32)
-                 for dx in range(3) for dy in range(3) for dz in range(3)], axis=0)
-            pre = dot(w2[...], patch) + b2
+        for y in range(8):
+            pre = pre2[j, y]
             t = jnp.tanh(0.5 * pre)
             slope = 0.65 + 0.35 * t + 0.175 * pre * (1.0 - t * t)
-            grad = (slope * cots[pl.ds(pl.multiple_of((y // 2) * 64, 64), 64), :]).astype(BF16)
-            rows = pl.ds(pl.multiple_of((y + 1) * 64, 64), 64)
-            gs[j + 1, rows] = grad[:, :128]
-            gs[j + 3, rows] = grad[:, 128:]
-            return 0
-
-        lax.fori_loop(0, 8, layer2, 0, unroll=True)
-
-    third = exchange(gs, (), 64, 16)
+            grad = (slope * cots[(y // 2) * 64:(y // 2) * 64 + 64, :]).astype(BF16)
+            gs[j + 1, (y + 2) * 64:(y + 3) * 64] = grad[:, :128]
+            gs[j + 3, (y + 2) * 64:(y + 3) * 64] = grad[:, 128:]
+
+    def depth_terms(part):
+        return part[32:64] + before2(part[64:96]) + after2(part[0:32])
+
+    for side, i, u in ((0, 1, 2), (1, 4, 0)):
+        for y in range(5):
+            patch = jnp.concatenate([gs[i, q * 64:q * 64 + 192] for q in (y, y + 5)], axis=1)
+            terms = dot(w2b[:, u * 192:u * 192 + 192], patch) * 0.125
+            xe[side, y * 32:y * 32 + 32] = depth_terms(terms[:, :128]).astype(BF16)
+            xe[side, (y + 5) * 32:(y + 6) * 32] = depth_terms(terms[:, 128:]).astype(BF16)
+
+    def back2(j, y):
+        patch = jnp.concatenate(
+            [jnp.concatenate([gs[i, (y + 1) * 64:(y + 4) * 64] for i in (j + u, j + u + 2)], axis=1) for u in range(3)],
+            axis=0)
+        terms = dot(w2b[...], patch) * 0.125
+        return depth_terms(terms[:, :128]), depth_terms(terms[:, 128:])
+
+    for side, y in ((0, -1), (1, 8)):
+        for j in range(2):
+            one, two = back2(j, y)
+            ye[side, j] = one.astype(BF16)
+            ye[side, j + 2] = two.astype(BF16)
+    third = []
+    for k, (sx, sy) in enumerate(DIRS):
+        a, b = (0 if sx == 1 else 1), (0 if sy == 1 else 1)
+        if sx == 0:
+            src, dst = ye.at[1 - b], rye.at[b]
+        elif sy == 0:
+            src, dst = xe.at[1 - a, pl.ds(32, 256)], rxe.at[a]
+        else:
+            src, dst = xe.at[1 - a, pl.ds(288 if sy == 1 else 0, 32)], rce.at[a, b]
+        third.append(remote(src, dst, 16 + k, at(sx, sy)))
+    start(third, (1, -1, 0))
+
+    def cell(ref, i, where, start, size):
+        rows = slice(start, start + size)
+        return jnp.concatenate([ref[(i,) + where + (rows,)], ref[(i + 2,) + where + (rows,)]], axis=1)
 
     for j in range(2):
-        def weights2(y, _, j=j):
-            grad = cell(gs, j + 1, (), pl.multiple_of((y + 1) * 64, 64), 64)
+        for y in range(8):
+            grad = cell(gs, j + 1, (), (y + 2) * 64, 64)
             for half in range(2):
                 patch = jnp.concatenate(
-                    [cell(pool, j + dx, (dz,), pl.multiple_of((y + dy) * 32 + half * 16, 16), 16)
+                    [cell(pool, j + dx, (dz,), (y + dy) * 32 + half * 16, 16)
                      for dx in range(3) for dy in range(3) for dz in range(3)], axis=0)
                 acc2[half, :, 0:432] += dot_nt(grad, patch)
-            return 0
-
-        lax.fori_loop(0, 8, weights2, 0, unroll=True)
     pair2 = remote(acc2.at[1 - dp], r2dp, 24, (gx, gy, 1 - dp))
     pair2.start()
-    for copy in third:
-        copy.wait()
-    clear(gs, (), 64)
-
     for j in range(2):
-        def back2(y, _, j=j):
-            patch = jnp.concatenate(
-                [cell(gs, j + u, (), pl.multiple_of(y * 64, 64), 192) for u in range(3)], axis=0)
-            terms = dot(w2b[...], patch) * 0.125
-            rows = pl.ds(pl.multiple_of(y * 32, 32), 32)
-            for h in range(2):
-                part = terms[:, h * 128:h * 128 + 128]
-                gp[j + 2 * h, rows] = part[32:64] + before2(part[64:96]) + after2(part[0:32])
-            return 0
-
-        lax.fori_loop(0, 8, back2, 0, unroll=True)
-
-    pair2.wait()
-    s2a[...] = (acc2[dp] + r2dp[...]).reshape(gxn, 8, 512)
-    along2 = []
-    for d in range(1, gxn):
-        along2.append(remote(s2a.at[lax.rem(gx + d, gxn)], r2gx.at[d - 1], 24 + d, at(d, 0)))
-        along2[-1].start()
+        for y in range(8):
+            one, two = back2(j, y)
+            gp[j, y * 32:y * 32 + 32] = one
+            gp[j + 2, y * 32:y * 32 + 32] = two
+    finish_all(third)
+
+    for a, ok, i in ((0, up, 0), (1, down, 3)):
+        gp[i] += jnp.where(ok, rxe[a].astype(F32), 0.0)
+        for b, ok2, r in ((0, left, 0), (1, right, 224)):
+            gp[i, r:r + 32] += jnp.where(jnp.logical_and(ok, ok2), rce[a, b].astype(F32), 0.0)
+    for b, ok, r in ((0, left, 0), (1, right, 224)):
+        for i in range(4):
+            gp[i, r:r + 32] += jnp.where(ok, rye[b, i].astype(F32), 0.0)
 
     for x in range(8):
         spread = gp[x // 2]
@@ -353,6 +430,13 @@
     for x in range(8):
         term = dot_nt(gf[x], xs[x:x + 3].reshape(720, 256))
         acc1[...] = term if x == 0 else acc1[...] + term
+
+    pair2.wait()
+    s2a[...] = (acc2[dp] + r2dp[...]).reshape(gxn, 8, 512)
+    along2 = []
+    for d in range(1, gxn):
+        along2.append(remote(s2a.at[lax.rem(gx + d, gxn)], r2gx.at[d - 1], 24 + d, at(d, 0)))
+        along2[-1].start()
 
     taps = None
     for dy in range(3):
@@ -367,19 +451,13 @@
         taps = parts if taps is None else taps + parts
     for g in range(8):
         s1[g] = taps[4 * g:4 * g + 4]
-    pair1 = remote(s1, r1dp, 48, (gx, gy, 1 - dp))
-    pair1.start()
-    for copy in along2:
-        copy.wait()
-    total2 = s2a[gx]
-    for d in range(1, gxn):
-        total2 = total2 + r2gx[d - 1]
-    for g in range(8):
-        s2b[g] = total2[g:g + 1]
-    across2 = []
-    for d in range(1, gyn):
-        across2.append(remote(s2b.at[lax.rem(gy + d, gyn)], r2gy.at[d - 1], 31 + d, at(0, d)))
-        across2[-1].start()
+    along1 = []
+    for d in range(gxn):
+        for e in range(2):
+            if d + e:
+                peer = (lax.rem(gx + d, gxn), gy, lax.rem(dp + e, 2))
+                along1.append(remote(s1.at[peer[0]], r1gx.at[2 * d + e - 1], 47 + 2 * d + e, peer))
+                along1[-1].start()
 
     for x in range(8):
         term = dot(w1tr[...], gf[x]).reshape(3, 240, 256)
@@ -388,13 +466,6 @@
         else:
             gi[x:x + 2] += term[:2]
             gi[x + 2] = term[2]
-        if x == 3:
-            pair1.wait()
-            s1a[...] = s1[...] + r1dp[...]
-            along1 = []
-            for d in range(1, gxn):
-                along1.append(remote(s1a.at[lax.rem(gx + d, gxn)], r1gx.at[d - 1], 48 + d, at(d, 0)))
-                along1[-1].start()
 
     def combine(x):
         return gi[x, 80:152] + before(gi[x, 160:232]) + after(gi[x, 0:72])
@@ -417,17 +488,49 @@
         else:
             src, dst = sc.at[1 if sx == 1 else 0], rc.at[a, b]
         fourth.append(remote(src, dst, 40 + k, at(sx, sy)))
-        fourth[-1].start()
+    start(fourth, (1, -1, 0))
     for copy in along1:
         copy.wait()
-    total1 = s1a[gx]
-    for d in range(1, gxn):
-        total1 = total1 + r1gx[d - 1]
+    total1 = s1[gx]
+    for i in range(2 * gxn - 1):
+        total1 = total1 + r1gx[i]
     s1b[...] = total1
     across1 = []
     for d in range(1, gyn):
-        across1.append(remote(s1b, r1gy.at[d - 1], 55 + d, at(0, d)))
+        across1.append(remote(s1b, r1gy.at[d - 1], 62 + d, at(0, d)))
         across1[-1].start()
+    for copy in along2:
+        copy.wait()
+    total2 = s2a[gx]
+    for d in range(1, gxn):
+        total2 = total2 + r2gx[d - 1]
+    for g in range(8):
+        s2b[g] = total2[g:g + 1]
+    across2 = []
+    for d in range(1, gyn):
+        across2.append(remote(s2b.at[lax.rem(gy + d, gyn)], r2gy.at[d - 1], 31 + d, at(0, d)))
+        across2[-1].start()
+    finish_all(fourth)
+    y16 = lax.broadcasted_iota(jnp.int32, (4, 16, 256), 1)
+
+    def ends(low_rows, high_rows):
+        low_part = jnp.where(jnp.logical_and(y16 == 0, left), low_rows[4:8][:, None, :], 0.0)
+        high_part = jnp.where(jnp.logical_and(y16 == 15, right), high_rows[0:4][:, None, :], 0.0)
+        return (low_part + high_part).reshape(64, 256)
+
+    for a, ok, x in ((0, up, 1), (1, down, 8)):
+        term = rx[a] + ends(rc[a, 0], rc[a, 1])
+        gi[x, 80:144] += jnp.where(ok, term, 0.0)
+
+    def finish(x, _):
+        total = (gi[x + 1, 80:144] + ends(ry[0, x], ry[1, x])).astype(BF16)
+        natural = dot(total, restore[...]).astype(BF16)
+        for n in range(2):
+            out[n, :, x] = natural[:, n * 128:n * 128 + 128].reshape(4, 16, 128)
+        return 0
+
+    lax.fori_loop(0, 8, finish, 0, unroll=True)
+
     for copy in across2:
         copy.wait()
     total2 = s2b[gy]
@@ -435,29 +538,6 @@
         total2 = total2 + r2gy[d - 1]
     total2 = jnp.concatenate([total2 * (1.0 / (CELLS / 8) ** 0.5)] * 8, axis=0)[:, :432]
     gw2[...] = split_dot(total2, reorder[...])[0:1]
-
-    for copy in fourth:
-        copy.wait()
-    y16 = lax.broadcasted_iota(jnp.int32, (4, 16, 256), 1)
-
-    def ends(low_rows, high_rows):
-        low_part = jnp.where(jnp.logical_and(y16 == 0, left), low_rows[4:8][:, None, :], 0.0)
-        high_part = jnp.where(jnp.logical_and(y16 == 15, right), high_rows[0:4][:, None, :], 0.0)
-        return (low_part + high_part).reshape(64, 256)
-
-    for a, ok, x in ((0, up, 1), (1, down, 8)):
-        term = rx[a] + ends(rc[a, 0], rc[a, 1])
-        gi[x, 80:144] += jnp.where(ok, term, 0.0)
-
-    def finish(x, _):
-        total = (gi[x + 1, 80:144] + ends(ry[0, x], ry[1, x])).astype(BF16)
-        natural = dot(total, restore[...]).astype(BF16)
-        for n in range(2):
-            out[n, :, x] = natural[:, n * 128:n * 128 + 128].reshape(4, 16, 128)
-        return 0
-
-    lax.fori_loop(0, 8, finish, 0, unroll=True)
-
     for copy in across1:
         copy.wait()
     total1 = s1b[...]
@@ -482,12 +562,14 @@
         ((10, 240, 256), BF16), ((8, 16, 256), BF16), ((2, 8, 16, 256), BF16), ((2, 2, 4, 16, 128), BF16),
         ((2, 2, 16, 256), BF16), ((512, 720), BF16), ((720, 512), BF16), ((64, 864), BF16), ((96, 576), BF16),
         ((128, 128), F32), ((128, 128), F32), ((8, 512, 256), F32), ((8, 512, 256), BF16), ((6, 3, 320, 128), BF16),
-        ((256, 256), F32), ((6, 640, 128), BF16), ((4, 256, 128), F32),
+        ((256, 256), F32), ((6, 768, 128), BF16), ((4, 256, 128), F32),
         ((2, 64, 512), F32), ((64, 512), F32), ((gxn, 8, 512), F32), ((gxn - 1, 8, 512), F32), ((gyn, 1, 512), F32),
         ((gyn - 1, 1, 512), F32), ((10, 240, 256), F32), ((8, 8, 256), F32), ((2, 8, 8, 256), F32),
         ((2, 64, 256), F32), ((2, 64, 256), F32), ((2, 8, 256), F32), ((2, 2, 8, 256), F32), ((512, 720), F32),
-        ((gxn, 4, 128), F32), ((gxn, 4, 128), F32), ((gxn, 4, 128), F32), ((gxn - 1, 4, 128), F32), ((4, 128), F32),
-        ((gyn - 1, 4, 128), F32), ((128, 32), F32),
+        ((gxn, 4, 128), F32), ((2 * gxn - 1, 4, 128), F32), ((4, 128), F32),
+        ((gyn - 1, 4, 128), F32), ((128, 32), F32), ((4, 64, 288), BF16), ((2, 8, 64, 256), F32),
+        ((2, 320, 128), BF16), ((2, 4, 32, 128), BF16), ((2, 256, 128), BF16), ((2, 4, 32, 128), BF16),
+        ((2, 2, 32, 128), BF16),
     ]
     result, part1, part2 = pl.pallas_call(
         functools.partial(kernel, gxn, gyn),
@@ -500,7 +582,7 @@
         out_specs=(vmem, vmem, vmem),
         scratch_shapes=[pltpu.VMEM(c.shape, c.dtype) for c in consts]
         + [pltpu.VMEM(s, d) for s, d in scratch]
-        + [pltpu.SemaphoreType.DMA((63,)), pltpu.SemaphoreType.DMA((63,)), pltpu.SemaphoreType.DMA((NCONST,))],
+        + [pltpu.SemaphoreType.DMA((70,)), pltpu.SemaphoreType.DMA((70,)), pltpu.SemaphoreType.DMA((NCONST,))],
         compiler_params=pltpu.CompilerParams(
             collective_id=0, has_side_effects=True, vmem_limit_bytes=60 * 1024 * 1024
         ),

time: 57.1 us -> 46.6 us (0.82)
  Pallas kernels: 53.5 us -> 42.6 us
    pallas_call x1, Pallas kernels: 53.5 us -> 42.6 us  [on_device(): pl.pallas_call(functools.partial(kernel, gxn, gyn), out_shape=(jax.ShapeD...]
where the time goes in v3:
time: 46.6 us; the launch traced here: 46 us
  Pallas kernels  42.6 us (91%)
  local copies, waits for them, and re-layouts  2.77 us (6%)
  between operations  0.66 us (1%)
    pallas_call x1, Pallas kernels, on_device(): pl.pallas_call(functools.partial(kernel, gxn, gyn), out_shape=(jax.ShapeD...  42.6 us
    unnamed x7, local copies, waits for them, and re-layouts  2.77 us

profile of v3, /device:TPU:0, one launch (start us, length us, event | category | flops | bytes accessed | tf_op | source)
XLA Modules:
  0.0 46.0 jit_solution(5883274594144579064)
XLA Ops:
  0.6 42.6 %shard_map.175 = (bf16[2,4,8,16,128]{4,3,2,1,0:T(8,128)(2,1)}, f32[1,27]{1,0:T(1,128)}, f32[1,432]{1,0:T(1,128)}) custom-call(bf16[2,4,8,16,128]{4,3,2,1,0:T(8,128)(2,1)} %inp.1, bf16[512,64]{1,0:T(8,128)(2,1)} %bitcast.14, bf16[27,4,32]{2,1,0:T(4,128)(2,1)} %bitcast.15, bf16[864,64]{1,0:T(8,128)(2,1)} %bitcast.13, f32[1,32]{1,0:T(1,128)} %bitcast.17, ...), custom_call_target="tpu_custom_call" | custom-call | tf_op jit(solution)/shard_map/pallas_call | solution.py:574
  43.2 0.0 copy-start.1
  43.2 0.0 copy-start
  43.2 1.7 %copy.22 = bf16[2,4,8,16,128]{4,3,2,1,0:T(8,128)(2,1)} copy(bf16[2,4,8,16,128]{4,3,2,1,0:T(8,128)(2,1)} %get-tuple-element.12) | data formatting | bytes 524288
  44.9 0.0 copy-done.1
  44.9 0.5 %copy.23 = f32[27]{0:T(128)} copy(f32[27]{0:T(128)S(1)} %bitcast.19) | data formatting | bytes 216
  45.4 0.0 copy-done
  45.4 0.6 %copy.24 = f32[432]{0:T(512)} copy(f32[432]{0:T(512)S(1)} %bitcast.16) | data formatting | bytes 3456
Async XLA Ops:
  43.2 1.7 %copy-start.1 = (f32[1,27]{1,0:T(1,128)S(1)}, f32[1,27]{1,0:T(1,128)}, u32[]{:S(2)}) copy-start(f32[1,27]{1,0:T(1,128)} %get-tuple-element.7) | copy-start | bytes 328
  43.2 2.2 %copy-start = (f32[1,432]{1,0:T(1,128)S(1)}, f32[1,432]{1,0:T(1,128)}, u32[]{:S(2)}) copy-start(f32[1,432]{1,0:T(1,128)} %get-tuple-element.8) | copy-start | bytes 5188

commit v4 on v3

--- a/solution.py
+++ b/solution.py
@@ -14,7 +14,7 @@
 BF16 = jnp.bfloat16
 DIRS = [(0, 1), (0, -1), (1, 0), (-1, 0), (1, 1), (1, -1), (-1, 1), (-1, -1)]
 CELLS = 4194304
-NCONST = 10
+NLOAD = 15
 
 
 def constants():
@@ -68,10 +68,12 @@
         select[c, c * 16 + 15] = 1
         select[4 + c, c * 16] = 1
     b16 = lambda v: v.astype(ml_dtypes.bfloat16)
-    return (
-        b16(depth_map), b16(restore), b16(pool_map), b16(cot_map), b16(toeplitz), b16(gather), b16(select),
-        b16(np.eye(128, dtype=np.float32)), b16(reorder), np.pad(np.tile(place, 9), (0, 48), constant_values=-100)[None, :],
-    )
+    place = np.pad(np.tile(place, 9), (0, 48), constant_values=-100)[None, :]
+    return {
+        "depth_map": b16(depth_map), "restore": b16(restore), "pool_map": b16(pool_map), "cot_map": b16(cot_map),
+        "toeplitz": b16(toeplitz), "gather": b16(gather), "select": b16(select), "reorder": b16(reorder),
+        "eye": b16(np.eye(128, dtype=np.float32)), "place": place,
+    }
 
 
 def dot(a, b):
@@ -116,15 +118,15 @@
 
 def kernel(
     gxn, gyn,
-    inp, cot, w1t, w2t, b1r, b2r, *rest):
-    fixed, rest = rest[:NCONST], rest[NCONST:]
+    *rest):
+    fixed, rest = rest[:NLOAD], rest[NLOAD:]
     out, gw1, gw2 = rest[:3]
-    kept, rest = rest[3:3 + NCONST], rest[3 + NCONST:]
+    kept, rest = rest[3:3 + NLOAD], rest[3 + NLOAD:]
     (xs, hb, hlr, hx, hc, w1, w1tr, w2, w2b, bias1, bias2, sl, gf, pool, cots, gs, gp,
     acc2, r2dp, s2a, r2gx, s2b, r2gy, gi, sby, ry, sx_, rx, sc, rc, acc1, s1, r1gx, s1b, r1gy,
     w1f, w2e, pre2, xe, ye, rxe, rye, rce, ssem, rsem, lsem) = rest
-    depth_map, restore, pool_map, cot_map, toeplitz, gather, select, eye, reorder, place = kept
-    loads = [pltpu.make_async_copy(fixed[i], kept[i], lsem.at[i]) for i in range(NCONST)]
+    inp, select, w1t, eye, toeplitz, place, depth_map, b1r, w2t, cot, b2r, pool_map, cot_map, gather, reorder = kept
+    loads = [pltpu.make_async_copy(fixed[i], kept[i], lsem.at[i]) for i in range(NLOAD)]
     for load in loads:
         load.start()
     gx, gy, dp = lax.axis_index("gx"), lax.axis_index("gy"), lax.axis_index("dp")
@@ -175,7 +177,8 @@
         halves = [inp[n, :, x].reshape(64, 128) for n in range(2)]
         return jnp.concatenate(halves, axis=1)
 
-    loads[6].wait()
+    loads[0].wait()
+    loads[1].wait()
     for x in range(8):
         hb[x] = dot(select[...], raw(x)).astype(BF16)
     pl.semaphore_wait(barrier, len(peers))
@@ -191,9 +194,8 @@
         first.append(remote(src, dst, k, at(sx, sy)))
     start(first, (1, -1, 0))
 
-    for i, load in enumerate(loads):
-        if i != 6:
-            load.wait()
+    for load in loads[2:8]:
+        load.wait()
     w1f[...] = jnp.zeros_like(w1f)
     for tap in range(27):
         w1f[tap * 4:tap * 4 + 4] = w1t[tap].astype(F32)
@@ -208,68 +210,33 @@
         if y == 15:
             block = block + base[:, 1536:]
         w1[r * 32:r * 32 + 32, :] = block[:, :720].astype(BF16)
-    for b in range(6):
-        width = min(128, 720 - b * 128)
-        w1tr[b * 128:b * 128 + width] = dot_nt(eye[:width, :width], w1[:, b * 128:b * 128 + width]).astype(BF16)
-    w2[...] = dot_nt(eye[:64, :64], w2t[...]).astype(BF16)
-    for dx in range(3):
-        for dy in range(3):
-            at_lane = ((2 - dx) * 3 + 2 - dy) * 64
-            row = (dx * 3 + dy) * 96
-            w2b[:, at_lane:at_lane + 64] = w2t[row:row + 96, :]
     bias1[...] = jnp.zeros_like(bias1)
     bias1[:, 0:32] = jnp.broadcast_to(b1r[...], (128, 32))
-    bias2[...] = jnp.zeros_like(bias2)
-    bias2[:, 0:64] = jnp.broadcast_to(b2r[...], (128, 64))
     b1 = jnp.transpose(bias1[...])[:32]
-    b2 = jnp.transpose(bias2[...])[:64]
     b1 = jnp.concatenate([b1, b1], axis=1)
-    b2 = jnp.concatenate([b2, b2], axis=1)
-    for q in range(4):
-        part = jnp.concatenate(
-            [cot[(n * 8 + h * 4 + q) * 32:(n * 8 + h * 4 + q) * 32 + 32, :] for n in range(2) for h in range(2)], axis=0
-        )
-        turned = dot_nt(eye[:64, :64], part).astype(BF16)
-        cots[q * 64:q * 64 + 64] = dot(turned, cot_map[...]) * 0.125
-
-    def slab(index, rows):
-        spread = dot(rows, depth_map[...]).astype(BF16)
+    spread = dot(jnp.concatenate([raw(x) for x in range(8)], axis=0), depth_map[...]).astype(BF16)
+    for x in range(8):
         for t in range(3):
-            xs[index, t * 80:t * 80 + 64] = spread[:, t * 256:t * 256 + 256]
-
-    for x in range(8):
-        slab(x + 1, raw(x))
-    acc2[...] = jnp.zeros_like(acc2)
-    for i in (0, 5):
-        gs[i] = jnp.zeros((768, 128), BF16)
-    for i in range(1, 5):
-        gs[i, 0:128] = jnp.zeros((128, 128), BF16)
-        gs[i, 640:768] = jnp.zeros((128, 128), BF16)
-    for i, picked in enumerate((
-        [(0, dy) for dy in range(3)], [(2, dy) for dy in range(3)], [(dx, 0) for dx in range(3)], [(dx, 2) for dx in range(3)]
-    )):
-        rows = [w2t[(dx * 3 + dy) * 96:(dx * 3 + dy) * 96 + 96, :] for dx, dy in picked]
-        w2e[i] = dot_nt(eye[:64, :64], jnp.concatenate(rows, axis=0)).astype(BF16)
+            xs[x + 1, t * 80:t * 80 + 64] = spread[x * 64:x * 64 + 64, t * 256:t * 256 + 256]
     finish_all(first)
     row16 = lax.broadcasted_iota(jnp.int32, (16, 256), 0)
     from_left = jnp.logical_and(row16 < 4, left)
     from_right = jnp.logical_and(jnp.logical_and(row16 >= 4, row16 < 8), right)
 
-    def halo(index, left_rows, right_rows, ok):
-        rows = jnp.where(from_left, left_rows.astype(F32), jnp.where(from_right, right_rows.astype(F32), 0.0))
-        if ok is not None:
-            rows = jnp.where(ok, rows, 0.0)
-        spread = dot(rows.astype(BF16), depth_map[...]).astype(BF16)
+    def halo(left_rows, right_rows):
+        return jnp.where(from_left, left_rows.astype(F32), jnp.where(from_right, right_rows.astype(F32), 0.0))
+
+    blocks = [halo(hlr[0, x], hlr[1, x]) for x in range(8)]
+    for a, ok in ((0, up), (1, down)):
+        rows = [hx[a, n].reshape(64, 128) for n in range(2)]
+        blocks.append(jnp.where(ok, jnp.concatenate(rows, axis=1).astype(F32), 0.0))
+        blocks.append(jnp.where(ok, halo(hc[a, 0], hc[a, 1]), 0.0))
+    spread = dot(jnp.concatenate(blocks, axis=0).astype(BF16), depth_map[...]).astype(BF16)
+    pieces = [(x + 1, 64, x * 16, 16) for x in range(8)]
+    pieces += [(0, 0, 128, 64), (0, 64, 192, 16), (9, 0, 208, 64), (9, 64, 272, 16)]
+    for index, row, at_row, size in pieces:
         for t in range(3):
-            xs[index, t * 80 + 64:t * 80 + 80] = spread[:, t * 256:t * 256 + 256]
-
-    for x in range(8):
-        halo(x + 1, hlr[0, x], hlr[1, x], None)
-    for a, ok in ((0, up), (1, down)):
-        index = 0 if a == 0 else 9
-        rows = jnp.concatenate([hx[a, n].reshape(64, 128) for n in range(2)], axis=1)
-        slab(index, jnp.where(ok, rows.astype(F32), 0.0).astype(BF16))
-        halo(index, hc[a, 0], hc[a, 1], ok)
+            xs[index, t * 80 + row:t * 80 + row + size] = spread[at_row:at_row + size, t * 256:t * 256 + 256]
 
     b1all = jnp.concatenate([b1] * 16, axis=0)
 
@@ -298,6 +265,18 @@
     layer1(2)
     start(second, (0,))
 
+    for load in loads[8:]:
+        load.wait()
+    w2[...] = dot_nt(eye[:64, :64], w2t[...]).astype(BF16)
+    for dx in range(3):
+        for dy in range(3):
+            at_lane = ((2 - dx) * 3 + 2 - dy) * 64
+            row = (dx * 3 + dy) * 96
+            w2b[:, at_lane:at_lane + 64] = w2t[row:row + 96, :]
+    bias2[...] = jnp.zeros_like(bias2)
+    bias2[:, 0:64] = jnp.broadcast_to(b2r[...], (128, 64))
+    b2 = jnp.transpose(bias2[...])[:64]
+    b2 = jnp.concatenate([b2, b2], axis=1)
     for i in range(1, 5):
         spread = dot(pool[i, 1, 32:288], pool_map[...]).astype(BF16)
         pool[i, 0, 32:288] = spread[:, :128]
@@ -316,6 +295,24 @@
                 [pair(j + dx, dz, y + dy) for dx in range(3) for dy in range(3) for dz in range(3)], axis=0)
             pre2[j, y] = dot(w2[...], patch) + b2
 
+    for q in range(4):
+        part = jnp.concatenate(
+            [cot[(n * 8 + h * 4 + q) * 32:(n * 8 + h * 4 + q) * 32 + 32, :] for n in range(2) for h in range(2)], axis=0
+        )
+        turned = dot_nt(eye[:64, :64], part).astype(BF16)
+        cots[q * 64:q * 64 + 64] = dot(turned, cot_map[...]) * 0.125
+
+    acc2[...] = jnp.zeros_like(acc2)
+    for i in (0, 5):
+        gs[i] = jnp.zeros((768, 128), BF16)
+    for i in range(1, 5):
+        gs[i, 0:128] = jnp.zeros((128, 128), BF16)
+        gs[i, 640:768] = jnp.zeros((128, 128), BF16)
+    for i, picked in enumerate((
+        [(0, dy) for dy in range(3)], [(2, dy) for dy in range(3)], [(dx, 0) for dx in range(3)], [(dx, 2) for dx in range(3)]
+    )):
+        rows = [w2t[(dx * 3 + dy) * 96:(dx * 3 + dy) * 96 + 96, :] for dx, dy in picked]
+        w2e[i] = dot_nt(eye[:64, :64], jnp.concatenate(rows, axis=0)).astype(BF16)
     finish_all(second)
     for ok, index in ((up, 0), (down, 5)):
         @pl.when(jnp.logical_not(ok))
@@ -412,6 +409,9 @@
             one, two = back2(j, y)
             gp[j, y * 32:y * 32 + 32] = one
             gp[j + 2, y * 32:y * 32 + 32] = two
+    for b in range(6):
+        width = min(128, 720 - b * 128)
+        w1tr[b * 128:b * 128 + width] = dot_nt(eye[:width, :width], w1[:, b * 128:b * 128 + width]).astype(BF16)
     finish_all(third)
 
     for a, ok, i in ((0, up, 0), (1, down, 3)):
@@ -522,14 +522,8 @@
         term = rx[a] + ends(rc[a, 0], rc[a, 1])
         gi[x, 80:144] += jnp.where(ok, term, 0.0)
 
-    def finish(x, _):
-        total = (gi[x + 1, 80:144] + ends(ry[0, x], ry[1, x])).astype(BF16)
-        natural = dot(total, restore[...]).astype(BF16)
-        for n in range(2):
-            out[n, :, x] = natural[:, n * 128:n * 128 + 128].reshape(4, 16, 128)
-        return 0
-
-    lax.fori_loop(0, 8, finish, 0, unroll=True)
+    for x in range(8):
+        out[x] = (gi[x + 1, 80:144] + ends(ry[0, x], ry[1, x])).astype(BF16)
 
     for copy in across2:
         copy.wait()
@@ -552,12 +546,26 @@
     gw1[...] = mine[:, 0:27] * (1.0 / CELLS ** 0.5)
 
 
+def write_back(total, restore, part1, part2, out, gw1, gw2):
+    natural = dot(total[...].reshape(512, 256), restore[...]).astype(BF16)
+    for x in range(8):
+        for n in range(2):
+            out[n, :, x] = natural[x * 64:x * 64 + 64, n * 128:n * 128 + 128].reshape(4, 16, 128)
+    gw1[...] = part1[...]
+    gw2[...] = part2[...]
+
+
 def on_device(gxn, gyn, consts, inputs, cotangent, w_first, w_second, b_first, b_second):
     cot = jnp.transpose(cotangent, (0, 2, 3, 4, 1)).reshape(512, 64)
     w1t = jnp.transpose(w_first, (2, 3, 4, 1, 0)).reshape(27, 4, 32)
     w2t = jnp.transpose(w_second, (2, 3, 4, 1, 0)).reshape(864, 64)
     vmem = pl.BlockSpec(memory_space=pltpu.VMEM)
-    operands = (inputs, cot, w1t, w2t, b_first.reshape(1, 32), b_second.reshape(1, 64), *consts)
+    b1, b2 = b_first.reshape(1, 32), b_second.reshape(1, 64)
+    c = {name: jnp.asarray(value) for name, value in consts.items()}
+    operands = (
+        inputs, c["select"], w1t, c["eye"], c["toeplitz"], c["place"], c["depth_map"], b1, w2t, cot, b2,
+        c["pool_map"], c["cot_map"], c["gather"], c["reorder"],
+    )
     scratch = [
         ((10, 240, 256), BF16), ((8, 16, 256), BF16), ((2, 8, 16, 256), BF16), ((2, 2, 4, 16, 128), BF16),
         ((2, 2, 16, 256), BF16), ((512, 720), BF16), ((720, 512), BF16), ((64, 864), BF16), ((96, 576), BF16),
@@ -571,22 +579,32 @@
         ((2, 320, 128), BF16), ((2, 4, 32, 128), BF16), ((2, 256, 128), BF16), ((2, 4, 32, 128), BF16),
         ((2, 2, 32, 128), BF16),
     ]
+    total, part1, part2 = pl.pallas_call(
+        functools.partial(kernel, gxn, gyn),
+        out_shape=(
+            jax.ShapeDtypeStruct((8, 64, 256), BF16),
+            jax.ShapeDtypeStruct((1, 27), F32),
+            jax.ShapeDtypeStruct((1, 432), F32),
+        ),
+        in_specs=[pl.BlockSpec(memory_space=pl.ANY)] * NLOAD,
+        out_specs=(vmem, vmem, vmem),
+        scratch_shapes=[pltpu.VMEM(v.shape, v.dtype) for v in operands]
+        + [pltpu.VMEM(s, d) for s, d in scratch]
+        + [pltpu.SemaphoreType.DMA((70,)), pltpu.SemaphoreType.DMA((70,)), pltpu.SemaphoreType.DMA((NLOAD,))],
+        compiler_params=pltpu.CompilerParams(
+            collective_id=0, has_side_effects=True, vmem_limit_bytes=60 * 1024 * 1024
+        ),
+    )(*operands)
     result, part1, part2 = pl.pallas_call(
-        functools.partial(kernel, gxn, gyn),
+        write_back,
         out_shape=(
             jax.ShapeDtypeStruct(inputs.shape, BF16),
             jax.ShapeDtypeStruct((1, 27), F32),
             jax.ShapeDtypeStruct((1, 432), F32),
         ),
-        in_specs=[vmem] * 6 + [pl.BlockSpec(memory_space=pl.ANY)] * NCONST,
+        in_specs=[vmem] * 4,
         out_specs=(vmem, vmem, vmem),
-        scratch_shapes=[pltpu.VMEM(c.shape, c.dtype) for c in consts]
-        + [pltpu.VMEM(s, d) for s, d in scratch]
-        + [pltpu.SemaphoreType.DMA((70,)), pltpu.SemaphoreType.DMA((70,)), pltpu.SemaphoreType.DMA((NCONST,))],
-        compiler_params=pltpu.CompilerParams(
-            collective_id=0, has_side_effects=True, vmem_limit_bytes=60 * 1024 * 1024
-        ),
-    )(*operands)
+    )(total, c["restore"], part1, part2)
     return result, part1.reshape(27), part2.reshape(432)
 
 

time: 46.6 us -> 44.2 us (0.948)
  local copies, waits for them, and re-layouts: 2.77 us -> 0 us
    unnamed x7 -> x0, local copies, waits for them, and re-layouts: 2.77 us -> none
    pallas_call x0 -> x1, Pallas kernels: none -> 1.97 us  [on_device(): pl.pallas_call(write_back, out_shape=(jax.ShapeDtypeStruct(inputs.shape,...]
    pallas_call x1, Pallas kernels: 42.6 us -> 41 us  [on_device(): pl.pallas_call(functools.partial(kernel, gxn, gyn), out_shape=(jax.ShapeD...]
where the time goes in v4:
time: 44.2 us; the launch traced here: 43.6 us
  Pallas kernels  42.9 us (97%)
  between operations  0.64 us (1%)
    pallas_call x1, Pallas kernels, on_device(): pl.pallas_call(functools.partial(kernel, gxn, gyn), out_shape=(jax.ShapeD...  41 us
    pallas_call x1, Pallas kernels, on_device(): pl.pallas_call(write_back, out_shape=(jax.ShapeDtypeStruct(inputs.shape,...  1.97 us

profile of v4, /device:TPU:0, one launch (start us, length us, event | category | flops | bytes accessed | tf_op | source)
XLA Modules:
  0.0 43.6 jit_solution(11451569407953236551)
XLA Ops:
  0.6 41.0 %shard_map.175 = (bf16[8,64,256]{2,1,0:T(8,128)(2,1)}, f32[1,27]{1,0:T(1,128)}, f32[1,432]{1,0:T(1,128)}) custom-call(bf16[2,4,8,16,128]{4,3,2,1,0:T(8,128)(2,1)} %rest_0_.1, bf16[16,64]{1,0:T(8,128)(2,1)} %constant.26.clone.rest_1_, bf16[27,4,32]{2,1,0:T(4,128)(2,1)} %bitcast.15, bf16[128,128]{1,0:T(8,128)(2,1)} %constant.28.clone.rest_3_, ...), custom_call_target="tpu_custom_call" | custom-call | tf_op jit(solution)/shard_map/pallas_call | solution.py:582
  41.6 2.0 %shard_map.176 = (bf16[2,4,8,16,128]{4,3,2,1,0:T(8,128)(2,1)}, f32[1,27]{1,0:T(1,128)}, f32[1,432]{1,0:T(1,128)}) custom-call(bf16[8,64,256]{2,1,0:T(8,128)(2,1)} %get-tuple-element.9.total, bf16[256,256]{1,0:T(8,128)(2,1)} %constant.21.clone.restore, f32[1,27]{1,0:T(1,128)} %get-tuple-element.10.part1, f32[1,432]{1,0:T(1,128)} %get-tuple-element.11.part2), custom_call_target="tpu_custom_call" | custom-call | tf_op jit(solution)/shard_map/pallas_call | solution.py:598

commit v5 on v4

--- a/solution.py
+++ b/solution.py
@@ -14,7 +14,7 @@
 BF16 = jnp.bfloat16
 DIRS = [(0, 1), (0, -1), (1, 0), (-1, 0), (1, 1), (1, -1), (-1, 1), (-1, -1)]
 CELLS = 4194304
-NLOAD = 15
+NLOAD = 18
 
 
 def constants():
@@ -63,15 +63,26 @@
     for tap in range(27):
         for c in range(16):
             reorder[tap * 16 + c, c * 27 + tap] = 1
-    select = np.zeros((16, 64), np.float32)
-    for c in range(4):
-        select[c, c * 16 + 15] = 1
-        select[4 + c, c * 16] = 1
+    select = np.zeros((64, 512), np.float32)
+    regroup = np.zeros((64, 64), np.float32)
+    expand = np.zeros((160, 128), np.float32)
+    for x in range(8):
+        for c in range(4):
+            select[x * 4 + c, x * 64 + c * 16 + 15] = 1
+            select[32 + x * 4 + c, x * 64 + c * 16] = 1
+            for side in range(2):
+                regroup[side * 32 + x * 4 + c, x * 8 + side * 4 + c] = 1
+                expand[x * 16 + side * 4 + c, side * 32 + x * 4 + c] = 1
+    for a in range(2):
+        for side in range(2):
+            for c in range(4):
+                expand[128 + a * 16 + side * 4 + c, 64 + a * 32 + side * 16 + (12 if a == 0 else 0) + c] = 1
     b16 = lambda v: v.astype(ml_dtypes.bfloat16)
     place = np.pad(np.tile(place, 9), (0, 48), constant_values=-100)[None, :]
     return {
         "depth_map": b16(depth_map), "restore": b16(restore), "pool_map": b16(pool_map), "cot_map": b16(cot_map),
         "toeplitz": b16(toeplitz), "gather": b16(gather), "select": b16(select), "reorder": b16(reorder),
+        "scatter": b16(select.T.copy()), "regroup": b16(regroup), "expand": b16(expand),
         "eye": b16(np.eye(128, dtype=np.float32)), "place": place,
     }
 
@@ -125,7 +136,8 @@
     (xs, hb, hlr, hx, hc, w1, w1tr, w2, w2b, bias1, bias2, sl, gf, pool, cots, gs, gp,
     acc2, r2dp, s2a, r2gx, s2b, r2gy, gi, sby, ry, sx_, rx, sc, rc, acc1, s1, r1gx, s1b, r1gy,
     w1f, w2e, pre2, xe, ye, rxe, rye, rce, ssem, rsem, lsem) = rest
-    inp, select, w1t, eye, toeplitz, place, depth_map, b1r, w2t, cot, b2r, pool_map, cot_map, gather, reorder = kept
+    inp, select, w1t, eye, toeplitz, place, depth_map, b1r, expand, w2t, cot, b2r, pool_map, cot_map, *others = kept
+    gather, reorder, regroup, scatter = others
     loads = [pltpu.make_async_copy(fixed[i], kept[i], lsem.at[i]) for i in range(NLOAD)]
     for load in loads:
         load.start()
@@ -179,22 +191,22 @@
 
     loads[0].wait()
     loads[1].wait()
-    for x in range(8):
-        hb[x] = dot(select[...], raw(x)).astype(BF16)
+    own = jnp.concatenate([raw(x) for x in range(8)], axis=0)
+    hb[...] = dot(select[...], own).astype(BF16)
     pl.semaphore_wait(barrier, len(peers))
     first = []
     for k, (sx, sy) in enumerate(DIRS):
         a, b = (0 if sx == 1 else 1), (0 if sy == 1 else 1)
         if sx == 0:
-            src, dst = hb, hlr.at[b]
+            src, dst = hb.at[pl.ds(b * 32, 32)], hlr.at[pl.ds(b * 32, 32)]
         elif sy == 0:
             src, dst = inp.at[:, :, 7 if sx == 1 else 0], hx.at[a]
         else:
-            src, dst = hb.at[7 if sx == 1 else 0], hc.at[a, b]
+            src, dst = hb.at[pl.ds(b * 32 + 16 - a * 16, 16)], hc.at[a, b]
         first.append(remote(src, dst, k, at(sx, sy)))
     start(first, (1, -1, 0))
 
-    for load in loads[2:8]:
+    for load in loads[2:9]:
         load.wait()
     w1f[...] = jnp.zeros_like(w1f)
     for tap in range(27):
@@ -214,23 +226,21 @@
     bias1[:, 0:32] = jnp.broadcast_to(b1r[...], (128, 32))
     b1 = jnp.transpose(bias1[...])[:32]
     b1 = jnp.concatenate([b1, b1], axis=1)
-    spread = dot(jnp.concatenate([raw(x) for x in range(8)], axis=0), depth_map[...]).astype(BF16)
+    spread = dot(own, depth_map[...]).astype(BF16)
     for x in range(8):
         for t in range(3):
             xs[x + 1, t * 80:t * 80 + 64] = spread[x * 64:x * 64 + 64, t * 256:t * 256 + 256]
     finish_all(first)
-    row16 = lax.broadcasted_iota(jnp.int32, (16, 256), 0)
-    from_left = jnp.logical_and(row16 < 4, left)
-    from_right = jnp.logical_and(jnp.logical_and(row16 >= 4, row16 < 8), right)
-
-    def halo(left_rows, right_rows):
-        return jnp.where(from_left, left_rows.astype(F32), jnp.where(from_right, right_rows.astype(F32), 0.0))
-
-    blocks = [halo(hlr[0, x], hlr[1, x]) for x in range(8)]
+    sides = [jnp.where(left, hlr[0:32].astype(F32), 0.0), jnp.where(right, hlr[32:64].astype(F32), 0.0)]
+    for a, ok in ((0, up), (1, down)):
+        for b, ok2 in ((0, left), (1, right)):
+            sides.append(jnp.where(jnp.logical_and(ok, ok2), hc[a, b].astype(F32), 0.0))
+    rims = dot(expand[...], jnp.concatenate(sides, axis=0).astype(BF16))
+    blocks = [rims[:128]]
     for a, ok in ((0, up), (1, down)):
         rows = [hx[a, n].reshape(64, 128) for n in range(2)]
         blocks.append(jnp.where(ok, jnp.concatenate(rows, axis=1).astype(F32), 0.0))
-        blocks.append(jnp.where(ok, halo(hc[a, 0], hc[a, 1]), 0.0))
+        blocks.append(rims[128 + a * 16:144 + a * 16])
     spread = dot(jnp.concatenate(blocks, axis=0).astype(BF16), depth_map[...]).astype(BF16)
     pieces = [(x + 1, 64, x * 16, 16) for x in range(8)]
     pieces += [(0, 0, 128, 64), (0, 64, 192, 16), (9, 0, 208, 64), (9, 64, 272, 16)]
@@ -265,7 +275,7 @@
     layer1(2)
     start(second, (0,))
 
-    for load in loads[8:]:
+    for load in loads[9:]:
         load.wait()
     w2[...] = dot_nt(eye[:64, :64], w2t[...]).astype(BF16)
     for dx in range(3):
@@ -422,21 +432,21 @@
         for i in range(4):
             gp[i, r:r + 32] += jnp.where(ok, rye[b, i].astype(F32), 0.0)
 
-    for x in range(8):
-        spread = gp[x // 2]
-        spread = jnp.concatenate([spread, spread], axis=1)
-        spread = jnp.concatenate([spread, spread], axis=0)
-        gf[x] = (sl[x] * spread).astype(BF16)
-    for x in range(8):
-        term = dot_nt(gf[x], xs[x:x + 3].reshape(720, 256))
-        acc1[...] = term if x == 0 else acc1[...] + term
-
     pair2.wait()
     s2a[...] = (acc2[dp] + r2dp[...]).reshape(gxn, 8, 512)
     along2 = []
     for d in range(1, gxn):
         along2.append(remote(s2a.at[lax.rem(gx + d, gxn)], r2gx.at[d - 1], 24 + d, at(d, 0)))
         along2[-1].start()
+
+    for x in range(8):
+        spread = gp[x // 2]
+        spread = jnp.concatenate([spread, spread], axis=1)
+        spread = jnp.concatenate([spread, spread], axis=0)
+        gf[x] = (sl[x] * spread).astype(BF16)
+    for x in range(8):
+        term = dot_nt(gf[x], xs[x:x + 3].reshape(720, 256))
+        acc1[...] = term if x == 0 else acc1[...] + term
 
     taps = None
     for dy in range(3):
@@ -459,6 +469,17 @@
                 along1.append(remote(s1.at[peer[0]], r1gx.at[2 * d + e - 1], 47 + 2 * d + e, peer))
                 along1[-1].start()
 
+    for copy in along2:
+        copy.wait()
+    total2 = s2a[gx]
+    for d in range(1, gxn):
+        total2 = total2 + r2gx[d - 1]
+    for g in range(8):
+        s2b[g] = total2[g:g + 1]
+    across2 = []
+    for d in range(1, gyn):
+        across2.append(remote(s2b.at[lax.rem(gy + d, gyn)], r2gy.at[d - 1], 31 + d, at(0, d)))
+        across2[-1].start()
     for x in range(8):
         term = dot(w1tr[...], gf[x]).reshape(3, 240, 256)
         if x == 0:
@@ -472,17 +493,19 @@
 
     for i, x in ((0, 0), (1, 9)):
         edge = combine(x)
-        sx_[i] = edge[:64]
-        sc[i] = edge[64:]
+        sx_[i] = edge[:64].astype(BF16)
+        sc[i] = jnp.concatenate([edge[64:], edge[64:]], axis=0).astype(BF16)
+    outer = []
     for x in range(8):
         inner = combine(x + 1)
         gi[x + 1, 80:144] = inner[:64]
-        sby[x] = inner[64:]
+        outer.append(inner[64:])
+    sby[...] = dot(regroup[...], jnp.concatenate(outer, axis=0).astype(BF16)).astype(BF16)
     fourth = []
     for k, (sx, sy) in enumerate(DIRS):
         a, b = (0 if sx == 1 else 1), (0 if sy == 1 else 1)
         if sx == 0:
-            src, dst = sby, ry.at[b]
+            src, dst = sby.at[pl.ds(32 - b * 32, 32)], ry.at[pl.ds(32 - b * 32, 32)]
         elif sy == 0:
             src, dst = sx_.at[1 if sx == 1 else 0], rx.at[a]
         else:
@@ -499,32 +522,6 @@
     for d in range(1, gyn):
         across1.append(remote(s1b, r1gy.at[d - 1], 62 + d, at(0, d)))
         across1[-1].start()
-    for copy in along2:
-        copy.wait()
-    total2 = s2a[gx]
-    for d in range(1, gxn):
-        total2 = total2 + r2gx[d - 1]
-    for g in range(8):
-        s2b[g] = total2[g:g + 1]
-    across2 = []
-    for d in range(1, gyn):
-        across2.append(remote(s2b.at[lax.rem(gy + d, gyn)], r2gy.at[d - 1], 31 + d, at(0, d)))
-        across2[-1].start()
-    finish_all(fourth)
-    y16 = lax.broadcasted_iota(jnp.int32, (4, 16, 256), 1)
-
-    def ends(low_rows, high_rows):
-        low_part = jnp.where(jnp.logical_and(y16 == 0, left), low_rows[4:8][:, None, :], 0.0)
-        high_part = jnp.where(jnp.logical_and(y16 == 15, right), high_rows[0:4][:, None, :], 0.0)
-        return (low_part + high_part).reshape(64, 256)
-
-    for a, ok, x in ((0, up, 1), (1, down, 8)):
-        term = rx[a] + ends(rc[a, 0], rc[a, 1])
-        gi[x, 80:144] += jnp.where(ok, term, 0.0)
-
-    for x in range(8):
-        out[x] = (gi[x + 1, 80:144] + ends(ry[0, x], ry[1, x])).astype(BF16)
-
     for copy in across2:
         copy.wait()
     total2 = s2b[gy]
@@ -532,6 +529,22 @@
         total2 = total2 + r2gy[d - 1]
     total2 = jnp.concatenate([total2 * (1.0 / (CELLS / 8) ** 0.5)] * 8, axis=0)[:, :432]
     gw2[...] = split_dot(total2, reorder[...])[0:1]
+    finish_all(fourth)
+    y16 = lax.broadcasted_iota(jnp.int32, (4, 16, 256), 1)
+
+    def ends(low_rows, high_rows):
+        low_part = jnp.where(jnp.logical_and(y16 == 0, left), low_rows[4:8][:, None, :], 0.0)
+        high_part = jnp.where(jnp.logical_and(y16 == 15, right), high_rows[0:4][:, None, :], 0.0)
+        return (low_part + high_part).reshape(64, 256)
+
+    for a, ok, x in ((0, up, 1), (1, down, 8)):
+        term = rx[a].astype(F32) + ends(rc[a, 0].astype(F32), rc[a, 1].astype(F32))
+        gi[x, 80:144] += jnp.where(ok, term, 0.0)
+    sides = [jnp.where(right, ry[0:32].astype(F32), 0.0), jnp.where(left, ry[32:64].astype(F32), 0.0)]
+    extra = dot(scatter[...], jnp.concatenate(sides, axis=0).astype(BF16))
+    for x in range(8):
+        out[x] = (gi[x + 1, 80:144] + extra[x * 64:x * 64 + 64]).astype(BF16)
+
     for copy in across1:
         copy.wait()
     total1 = s1b[...]
@@ -563,17 +576,17 @@
     b1, b2 = b_first.reshape(1, 32), b_second.reshape(1, 64)
     c = {name: jnp.asarray(value) for name, value in consts.items()}
     operands = (
-        inputs, c["select"], w1t, c["eye"], c["toeplitz"], c["place"], c["depth_map"], b1, w2t, cot, b2,
-        c["pool_map"], c["cot_map"], c["gather"], c["reorder"],
+        inputs, c["select"], w1t, c["eye"], c["toeplitz"], c["place"], c["depth_map"], b1, c["expand"], w2t, cot, b2,
+        c["pool_map"], c["cot_map"], c["gather"], c["reorder"], c["regroup"], c["scatter"],
     )
     scratch = [
-        ((10, 240, 256), BF16), ((8, 16, 256), BF16), ((2, 8, 16, 256), BF16), ((2, 2, 4, 16, 128), BF16),
+        ((10, 240, 256), BF16), ((64, 256), BF16), ((64, 256), BF16), ((2, 2, 4, 16, 128), BF16),
         ((2, 2, 16, 256), BF16), ((512, 720), BF16), ((720, 512), BF16), ((64, 864), BF16), ((96, 576), BF16),
         ((128, 128), F32), ((128, 128), F32), ((8, 512, 256), F32), ((8, 512, 256), BF16), ((6, 3, 320, 128), BF16),
         ((256, 256), F32), ((6, 768, 128), BF16), ((4, 256, 128), F32),
         ((2, 64, 512), F32), ((64, 512), F32), ((gxn, 8, 512), F32), ((gxn - 1, 8, 512), F32), ((gyn, 1, 512), F32),
-        ((gyn - 1, 1, 512), F32), ((10, 240, 256), F32), ((8, 8, 256), F32), ((2, 8, 8, 256), F32),
-        ((2, 64, 256), F32), ((2, 64, 256), F32), ((2, 8, 256), F32), ((2, 2, 8, 256), F32), ((512, 720), F32),
+        ((gyn - 1, 1, 512), F32), ((10, 240, 256), F32), ((64, 256), BF16), ((64, 256), BF16),
+        ((2, 64, 256), BF16), ((2, 64, 256), BF16), ((2, 16, 256), BF16), ((2, 2, 16, 256), BF16), ((512, 720), F32),
         ((gxn, 4, 128), F32), ((2 * gxn - 1, 4, 128), F32), ((4, 128), F32),
         ((gyn - 1, 4, 128), F32), ((128, 32), F32), ((4, 64, 288), BF16), ((2, 8, 64, 256), F32),
         ((2, 320, 128), BF16), ((2, 4, 32, 128), BF16), ((2, 256, 128), BF16), ((2, 4, 32, 128), BF16),

time: 44.2 us -> 43.7 us (0.989)
  no operation moved by 1% of the time
where the time goes in v5:
time: 43.7 us; the launch traced here: 43.2 us
  Pallas kernels  42.6 us (97%)
  between operations  0.64 us (1%)
    pallas_call x1, Pallas kernels, on_device(): pl.pallas_call(functools.partial(kernel, gxn, gyn), out_shape=(jax.ShapeD...  40.6 us
    pallas_call x1, Pallas kernels, on_device(): pl.pallas_call(write_back, out_shape=(jax.ShapeDtypeStruct(inputs.shape,...  1.96 us

profile of v5, /device:TPU:0, one launch (start us, length us, event | category | flops | bytes accessed | tf_op | source)
XLA Modules:
  0.0 43.2 jit_solution(16491554772023971875)
XLA Ops:
  0.6 40.6 %shard_map.202 = (bf16[8,64,256]{2,1,0:T(8,128)(2,1)}, f32[1,27]{1,0:T(1,128)}, f32[1,432]{1,0:T(1,128)}) custom-call(bf16[2,4,8,16,128]{4,3,2,1,0:T(8,128)(2,1)} %rest_0_.1, bf16[64,512]{1,0:T(8,128)(2,1)} %constant.32.clone.rest_1_, bf16[27,4,32]{2,1,0:T(4,128)(2,1)} %bitcast.15, bf16[128,128]{1,0:T(8,128)(2,1)} %constant.37.clone.rest_3_, ...), custom_call_target="tpu_custom_call" | custom-call | tf_op jit(solution)/shard_map/pallas_call | solution.py:595
  41.2 2.0 %shard_map.203 = (bf16[2,4,8,16,128]{4,3,2,1,0:T(8,128)(2,1)}, f32[1,27]{1,0:T(1,128)}, f32[1,432]{1,0:T(1,128)}) custom-call(bf16[8,64,256]{2,1,0:T(8,128)(2,1)} %get-tuple-element.9.total, bf16[256,256]{1,0:T(8,128)(2,1)} %constant.27.clone.restore, f32[1,27]{1,0:T(1,128)} %get-tuple-element.10.part1, f32[1,432]{1,0:T(1,128)} %get-tuple-element.11.part2), custom_call_target="tpu_custom_call" | custom-call | tf_op jit(solution)/shard_map/pallas_call | solution.py:611

commit v6 on v5

--- a/solution.py
+++ b/solution.py
@@ -139,7 +139,7 @@
     inp, select, w1t, eye, toeplitz, place, depth_map, b1r, expand, w2t, cot, b2r, pool_map, cot_map, *others = kept
     gather, reorder, regroup, scatter = others
     loads = [pltpu.make_async_copy(fixed[i], kept[i], lsem.at[i]) for i in range(NLOAD)]
-    for load in loads:
+    for load in loads[:2]:
         load.start()
     gx, gy, dp = lax.axis_index("gx"), lax.axis_index("gy"), lax.axis_index("dp")
 
@@ -184,27 +184,43 @@
     peers += [(lax.rem(gx + d, gxn), gy, 1 - dp) for d in range(gxn)]
     for peer in peers:
         pl.semaphore_signal(barrier, inc=1, device_id=peer, device_id_type=MESH)
+    for load in loads[2:]:
+        load.start()
 
     def raw(x):
         halves = [inp[n, :, x].reshape(64, 128) for n in range(2)]
         return jnp.concatenate(halves, axis=1)
 
+    pl.semaphore_wait(barrier, len(peers))
+    faces = []
+    for k, sx in ((2, 1), (3, -1)):
+        faces.append(remote(fixed[0].at[:, :, 7 if sx == 1 else 0], hx.at[0 if sx == 1 else 1], k, at(sx, 0)))
+    for copy, ok in zip(faces, (down, up)):
+        @pl.when(ok)
+        def _(copy=copy):
+            copy.start()
     loads[0].wait()
     loads[1].wait()
     own = jnp.concatenate([raw(x) for x in range(8)], axis=0)
     hb[...] = dot(select[...], own).astype(BF16)
-    pl.semaphore_wait(barrier, len(peers))
     first = []
     for k, (sx, sy) in enumerate(DIRS):
         a, b = (0 if sx == 1 else 1), (0 if sy == 1 else 1)
         if sx == 0:
             src, dst = hb.at[pl.ds(b * 32, 32)], hlr.at[pl.ds(b * 32, 32)]
         elif sy == 0:
-            src, dst = inp.at[:, :, 7 if sx == 1 else 0], hx.at[a]
+            first.append(faces[a])
+            continue
         else:
             src, dst = hb.at[pl.ds(b * 32 + 16 - a * 16, 16)], hc.at[a, b]
         first.append(remote(src, dst, k, at(sx, sy)))
-    start(first, (1, -1, 0))
+    start(first, (0,))
+    for sx, ok in ((1, down), (-1, up)):
+        @pl.when(ok)
+        def _(sx=sx):
+            for copy, d in zip(first, DIRS):
+                if d[0] == sx and d[1]:
+                    copy.start()
 
     for load in loads[2:9]:
         load.wait()
@@ -469,17 +485,6 @@
                 along1.append(remote(s1.at[peer[0]], r1gx.at[2 * d + e - 1], 47 + 2 * d + e, peer))
                 along1[-1].start()
 
-    for copy in along2:
-        copy.wait()
-    total2 = s2a[gx]
-    for d in range(1, gxn):
-        total2 = total2 + r2gx[d - 1]
-    for g in range(8):
-        s2b[g] = total2[g:g + 1]
-    across2 = []
-    for d in range(1, gyn):
-        across2.append(remote(s2b.at[lax.rem(gy + d, gyn)], r2gy.at[d - 1], 31 + d, at(0, d)))
-        across2[-1].start()
     for x in range(8):
         term = dot(w1tr[...], gf[x]).reshape(3, 240, 256)
         if x == 0:
@@ -522,6 +527,33 @@
     for d in range(1, gyn):
         across1.append(remote(s1b, r1gy.at[d - 1], 62 + d, at(0, d)))
         across1[-1].start()
+    for copy in along2:
+        copy.wait()
+    total2 = s2a[gx]
+    for d in range(1, gxn):
+        total2 = total2 + r2gx[d - 1]
+    for g in range(8):
+        s2b[g] = total2[g:g + 1]
+    across2 = []
+    for d in range(1, gyn):
+        across2.append(remote(s2b.at[lax.rem(gy + d, gyn)], r2gy.at[d - 1], 31 + d, at(0, d)))
+        across2[-1].start()
+    finish_all(fourth)
+    y16 = lax.broadcasted_iota(jnp.int32, (4, 16, 256), 1)
+
+    def ends(low_rows, high_rows):
+        low_part = jnp.where(jnp.logical_and(y16 == 0, left), low_rows[4:8][:, None, :], 0.0)
+        high_part = jnp.where(jnp.logical_and(y16 == 15, right), high_rows[0:4][:, None, :], 0.0)
+        return (low_part + high_part).reshape(64, 256)
+
+    for a, ok, x in ((0, up, 1), (1, down, 8)):
+        term = rx[a].astype(F32) + ends(rc[a, 0].astype(F32), rc[a, 1].astype(F32))
+        gi[x, 80:144] += jnp.where(ok, term, 0.0)
+    sides = [jnp.where(right, ry[0:32].astype(F32), 0.0), jnp.where(left, ry[32:64].astype(F32), 0.0)]
+    extra = dot(scatter[...], jnp.concatenate(sides, axis=0).astype(BF16))
+    for x in range(8):
+        out[x] = (gi[x + 1, 80:144] + extra[x * 64:x * 64 + 64]).astype(BF16)
+
     for copy in across2:
         copy.wait()
     total2 = s2b[gy]
@@ -529,22 +561,6 @@
         total2 = total2 + r2gy[d - 1]
     total2 = jnp.concatenate([total2 * (1.0 / (CELLS / 8) ** 0.5)] * 8, axis=0)[:, :432]
     gw2[...] = split_dot(total2, reorder[...])[0:1]
-    finish_all(fourth)
-    y16 = lax.broadcasted_iota(jnp.int32, (4, 16, 256), 1)
-
-    def ends(low_rows, high_rows):
-        low_part = jnp.where(jnp.logical_and(y16 == 0, left), low_rows[4:8][:, None, :], 0.0)
-        high_part = jnp.where(jnp.logical_and(y16 == 15, right), high_rows[0:4][:, None, :], 0.0)
-        return (low_part + high_part).reshape(64, 256)
-
-    for a, ok, x in ((0, up, 1), (1, down, 8)):
-        term = rx[a].astype(F32) + ends(rc[a, 0].astype(F32), rc[a, 1].astype(F32))
-        gi[x, 80:144] += jnp.where(ok, term, 0.0)
-    sides = [jnp.where(right, ry[0:32].astype(F32), 0.0), jnp.where(left, ry[32:64].astype(F32), 0.0)]
-    extra = dot(scatter[...], jnp.concatenate(sides, axis=0).astype(BF16))
-    for x in range(8):
-        out[x] = (gi[x + 1, 80:144] + extra[x * 64:x * 64 + 64]).astype(BF16)
-
     for copy in across1:
         copy.wait()
     total1 = s1b[...]

time: 43.7 us -> 42.8 us (0.979)
  Pallas kernels: 42.6 us -> 41.6 us
    pallas_call x1, Pallas kernels: 40.6 us -> 39.6 us  [on_device(): pl.pallas_call(functools.partial(kernel, gxn, gyn), out_shape=(jax.ShapeD...]
where the time goes in v6:
time: 42.8 us; the launch traced here: 42.2 us
  Pallas kernels  41.6 us (97%)
  between operations  0.64 us (1%)
    pallas_call x1, Pallas kernels, on_device(): pl.pallas_call(functools.partial(kernel, gxn, gyn), out_shape=(jax.ShapeD...  39.6 us
    pallas_call x1, Pallas kernels, on_device(): pl.pallas_call(write_back, out_shape=(jax.ShapeDtypeStruct(inputs.shape,...  1.96 us

profile of v6, /device:TPU:0, one launch (start us, length us, event | category | flops | bytes accessed | tf_op | source)
XLA Modules:
  0.0 42.2 jit_solution(5971979020721406354)
XLA Ops:
  0.6 39.6 %shard_map.202 = (bf16[8,64,256]{2,1,0:T(8,128)(2,1)}, f32[1,27]{1,0:T(1,128)}, f32[1,432]{1,0:T(1,128)}) custom-call(bf16[2,4,8,16,128]{4,3,2,1,0:T(8,128)(2,1)} %rest_0_.1, bf16[64,512]{1,0:T(8,128)(2,1)} %constant.32.clone.rest_1_, bf16[27,4,32]{2,1,0:T(4,128)(2,1)} %bitcast.15, bf16[128,128]{1,0:T(8,128)(2,1)} %constant.37.clone.rest_3_, ...), custom_call_target="tpu_custom_call" | custom-call | tf_op jit(solution)/shard_map/pallas_call | solution.py:611
  40.3 2.0 %shard_map.203 = (bf16[2,4,8,16,128]{4,3,2,1,0:T(8,128)(2,1)}, f32[1,27]{1,0:T(1,128)}, f32[1,432]{1,0:T(1,128)}) custom-call(bf16[8,64,256]{2,1,0:T(8,128)(2,1)} %get-tuple-element.9.total, bf16[256,256]{1,0:T(8,128)(2,1)} %constant.27.clone.restore, f32[1,27]{1,0:T(1,128)} %get-tuple-element.10.part1, f32[1,432]{1,0:T(1,128)} %get-tuple-element.11.part2), custom_call_target="tpu_custom_call" | custom-call | tf_op jit(solution)/shard_map/pallas_call | solution.py:627

commit v7 on v6

--- a/solution.py
+++ b/solution.py
@@ -460,6 +460,7 @@
         spread = jnp.concatenate([spread, spread], axis=1)
         spread = jnp.concatenate([spread, spread], axis=0)
         gf[x] = (sl[x] * spread).astype(BF16)
+
     for x in range(8):
         term = dot_nt(gf[x], xs[x:x + 3].reshape(720, 256))
         acc1[...] = term if x == 0 else acc1[...] + term
@@ -485,27 +486,24 @@
                 along1.append(remote(s1.at[peer[0]], r1gx.at[2 * d + e - 1], 47 + 2 * d + e, peer))
                 along1[-1].start()
 
-    for x in range(8):
-        term = dot(w1tr[...], gf[x]).reshape(3, 240, 256)
-        if x == 0:
-            gi[0:3] = term
-        else:
-            gi[x:x + 2] += term[:2]
-            gi[x + 2] = term[2]
-
-    def combine(x):
-        return gi[x, 80:152] + before(gi[x, 160:232]) + after(gi[x, 0:72])
-
-    for i, x in ((0, 0), (1, 9)):
-        edge = combine(x)
-        sx_[i] = edge[:64].astype(BF16)
-        sc[i] = jnp.concatenate([edge[64:], edge[64:]], axis=0).astype(BF16)
-    outer = []
-    for x in range(8):
-        inner = combine(x + 1)
-        gi[x + 1, 80:144] = inner[:64]
-        outer.append(inner[64:])
-    sby[...] = dot(regroup[...], jnp.concatenate(outer, axis=0).astype(BF16)).astype(BF16)
+    rows = [w1tr[g * 80 + 64:g * 80 + 80, :] for g in range(9)]
+    rows = jnp.concatenate(rows, axis=0)
+    rows = jnp.concatenate([rows[:, 0:32], rows[:, 480:512]], axis=1)
+    ends_of = [dot(rows, jnp.concatenate([gf[x, 0:32], gf[x, 480:512]], axis=0)) for x in range(8)]
+    depth = []
+    for dz in range(3):
+        sums = []
+        for i in range(10):
+            parts = [ends_of[i - dx][(dx * 3 + dz) * 16:(dx * 3 + dz) * 16 + 8] for dx in range(3) if 0 <= i - dx < 8]
+            sums.append(functools.reduce(lambda p, q: p + q, parts))
+        depth.append(jnp.concatenate(sums, axis=0))
+    outer = depth[1] + before(depth[2]) + after(depth[0])
+    sby[...] = dot(regroup[...], outer[8:72].astype(BF16)).astype(BF16)
+    for i, x, dx in ((0, 0, 0), (1, 7, 2)):
+        face = dot(w1tr[dx * 240:dx * 240 + 240], gf[x])
+        sx_[i] = (face[80:144] + before(face[160:224]) + after(face[0:64])).astype(BF16)
+        corner = outer[i * 72:i * 72 + 8]
+        sc[i] = jnp.concatenate([corner, corner], axis=0).astype(BF16)
     fourth = []
     for k, (sx, sy) in enumerate(DIRS):
         a, b = (0 if sx == 1 else 1), (0 if sy == 1 else 1)
@@ -517,6 +515,17 @@
             src, dst = sc.at[1 if sx == 1 else 0], rc.at[a, b]
         fourth.append(remote(src, dst, 40 + k, at(sx, sy)))
     start(fourth, (1, -1, 0))
+
+    for x in range(8):
+        term = dot(w1tr[...], gf[x]).reshape(3, 240, 256)
+        if x == 0:
+            gi[0:3] = term
+        else:
+            gi[x:x + 2] += term[:2]
+            gi[x + 2] = term[2]
+
+    for x in range(8):
+        gi[x + 1, 80:144] += before(gi[x + 1, 160:224]) + after(gi[x + 1, 0:64])
     for copy in along1:
         copy.wait()
     total1 = s1[gx]

time: 42.8 us -> 42.8 us (level)
  no operation moved by 1% of the time
where the time goes in v7:
time: 42.8 us; the launch traced here: 42.2 us
  Pallas kernels  41.6 us (97%)
  between operations  0.64 us (1%)
    pallas_call x1, Pallas kernels, on_device(): pl.pallas_call(functools.partial(kernel, gxn, gyn), out_shape=(jax.ShapeD...  39.6 us
    pallas_call x1, Pallas kernels, on_device(): pl.pallas_call(write_back, out_shape=(jax.ShapeDtypeStruct(inputs.shape,...  1.96 us

profile of v7, /device:TPU:0, one launch (start us, length us, event | category | flops | bytes accessed | tf_op | source)
XLA Modules:
  0.0 42.2 jit_solution(10976171160160572746)
XLA Ops:
  0.6 39.6 %shard_map.202 = (bf16[8,64,256]{2,1,0:T(8,128)(2,1)}, f32[1,27]{1,0:T(1,128)}, f32[1,432]{1,0:T(1,128)}) custom-call(bf16[2,4,8,16,128]{4,3,2,1,0:T(8,128)(2,1)} %rest_0_.1, bf16[64,512]{1,0:T(8,128)(2,1)} %constant.32.clone.rest_1_, bf16[27,4,32]{2,1,0:T(4,128)(2,1)} %bitcast.15, bf16[128,128]{1,0:T(8,128)(2,1)} %constant.37.clone.rest_3_, ...), custom_call_target="tpu_custom_call" | custom-call | tf_op jit(solution)/shard_map/pallas_call | solution.py:620
  40.2 2.0 %shard_map.203 = (bf16[2,4,8,16,128]{4,3,2,1,0:T(8,128)(2,1)}, f32[1,27]{1,0:T(1,128)}, f32[1,432]{1,0:T(1,128)}) custom-call(bf16[8,64,256]{2,1,0:T(8,128)(2,1)} %get-tuple-element.9.total, bf16[256,256]{1,0:T(8,128)(2,1)} %constant.27.clone.restore, f32[1,27]{1,0:T(1,128)} %get-tuple-element.10.part1, f32[1,432]{1,0:T(1,128)} %get-tuple-element.11.part2), custom_call_target="tpu_custom_call" | custom-call | tf_op jit(solution)/shard_map/pallas_call | solution.py:636
